TPU v7x, 128 devices: a whole 4x4x4 slice. The times are simulated.
128 devices in a mesh: ctx: 4 (over y), head: 32 (over x, z, core).
Axes of the slice: x: 4, y: 4, z: 4, core: 2. Of those that a mesh axis runs over, the one named last changes fastest.
Arguments:
- queries: bfloat16 [16384, 4096], P(('ctx', 'head')), may hold values from -24 to 24
- keys: bfloat16 [16384, 1024], P(('ctx', 'head')), may hold values from -10 to 10
- values: bfloat16 [16384, 1024], P(('ctx', 'head')), may hold values from -6 to 6
Outputs:
- attended: bfloat16 [16384, 4096], P(('ctx', 'head'))
All inputs are finite; a program needn't handle non-finite values.
Results may differ from a plain program's by a relative error of at most 0.0049.
Values may be sent and summed in bfloat16 or wider, within the bound.
A program may use at most 192 MiB of HBM per device.

v0:
```python
import math

import jax
import jax.numpy as jnp
from jax import lax
from jax.sharding import PartitionSpec as P

KEY_VALUE_HEADS = 8
HEAD_WIDTH = 128
TILE_ROWS = 1024


def attend(carry_state, q_rows, k_rows, v_rows, q_first, k_first, masked):
    maxima, totals, accumulated = carry_state
    row_count = q_rows.shape[0]
    key_count = k_rows.shape[0]
    kv_local = k_rows.shape[1] // HEAD_WIDTH
    per_kv = q_rows.shape[1] // HEAD_WIDTH // kv_local
    q_heads = q_rows.reshape(row_count, kv_local, per_kv, HEAD_WIDTH)
    k_heads = k_rows.reshape(key_count, kv_local, HEAD_WIDTH)
    v_heads = v_rows.reshape(key_count, kv_local, HEAD_WIDTH)
    scores = jnp.einsum(
        "rkgd,tkd->rkgt", q_heads, k_heads, preferred_element_type=jnp.float32
    ) * HEAD_WIDTH ** (-0.5)
    if masked:
        q_pos = q_first + jnp.arange(row_count, dtype=jnp.int32)
        k_pos = k_first + jnp.arange(key_count, dtype=jnp.int32)
        allowed = (q_pos[:, None] >= k_pos[None, :])[:, None, None, :]
        scores = jnp.where(allowed, scores, jnp.float32(-1e30))
    old_peak = maxima.reshape(row_count, kv_local, per_kv)
    new_peak = jnp.maximum(old_peak, jnp.max(scores, axis=-1))
    weights = jnp.exp(scores - new_peak[..., None])
    if masked:
        weights = jnp.where(allowed, weights, jnp.float32(0.0))
    rescale = jnp.exp(old_peak - new_peak)
    new_totals = totals.reshape(row_count, kv_local, per_kv) * rescale + jnp.sum(weights, axis=-1)
    mixture = jnp.einsum(
        "rkgt,tkd->rkgd", weights.astype(jnp.bfloat16), v_heads, preferred_element_type=jnp.float32
    )
    new_acc = (
        accumulated.reshape(row_count, kv_local, per_kv, HEAD_WIDTH) * rescale[..., None] + mixture
    )
    return (
        new_peak.reshape(row_count, -1),
        new_totals.reshape(row_count, -1),
        new_acc.reshape(row_count, -1),
    )


def causal_block(carry_state, q_block, k_block, v_block, q_base):
    tile = math.gcd(TILE_ROWS, q_block.shape[0])
    q_tiles = q_block.shape[0] // tile
    key_count = k_block.shape[0]
    key_tile = math.gcd(TILE_ROWS, key_count)
    key_tiles = key_count // key_tile

    def over_queries(tile_index, carry):
        q_first = q_base + tile_index * tile
        section = tuple(
            (lax.dynamic_slice_in_dim(item, tile_index * tile, tile, 0) for item in carry)
        )
        q_tile = lax.dynamic_slice_in_dim(q_block, tile_index * tile, tile, 0)

        def over_keys(key_index, state):
            k_first = key_index * key_tile
            k_tile = lax.dynamic_slice_in_dim(k_block, key_index * key_tile, key_tile, 0)
            v_tile = lax.dynamic_slice_in_dim(v_block, key_index * key_tile, key_tile, 0)
            which = jnp.where(k_first + key_tile <= q_first, 0, 1).astype(jnp.int32)
            return lax.switch(
                which,
                [
                    lambda inner: attend(inner, q_tile, k_tile, v_tile, q_first, k_first, False),
                    lambda inner: attend(inner, q_tile, k_tile, v_tile, q_first, k_first, True),
                ],
                state,
            )

        needed = jnp.clip((q_first + tile + key_tile - 1) // key_tile, 0, key_tiles)
        section = lax.fori_loop(jnp.int32(0), needed, over_keys, section)
        return tuple(
            (
                lax.dynamic_update_slice_in_dim(item, piece, tile_index * tile, 0)
                for item, piece in zip(carry, section)
            )
        )

    return lax.fori_loop(0, q_tiles, over_queries, carry_state)


def empty_state(row_count, q_width):
    heads_here = q_width // HEAD_WIDTH
    return (
        jnp.full((row_count, heads_here), -1e30, jnp.float32),
        jnp.zeros((row_count, heads_here), jnp.float32),
        jnp.zeros((row_count, q_width), jnp.float32),
    )


def per_device(queries, keys, values):
    head_shard_axis = lax.axis_size("head")
    token_rows = queries.shape[0]
    repeat_heads = max(1, head_shard_axis // KEY_VALUE_HEADS)
    k_wide = jnp.broadcast_to(
        keys.reshape(token_rows, KEY_VALUE_HEADS, 1, HEAD_WIDTH),
        (token_rows, KEY_VALUE_HEADS, repeat_heads, HEAD_WIDTH),
    ).reshape(token_rows, -1)
    v_wide = jnp.broadcast_to(
        values.reshape(token_rows, KEY_VALUE_HEADS, 1, HEAD_WIDTH),
        (token_rows, KEY_VALUE_HEADS, repeat_heads, HEAD_WIDTH),
    ).reshape(token_rows, -1)
    q_here, k_here, v_here = (
        lax.all_to_all(queries, "head", split_axis=1, concat_axis=0, tiled=True),
        lax.all_to_all(k_wide, "head", split_axis=1, concat_axis=0, tiled=True),
        lax.all_to_all(v_wide, "head", split_axis=1, concat_axis=0, tiled=True),
    )
    group = q_here.shape[0]
    q_width = q_here.shape[1]
    own_base = lax.axis_index("ctx") * group
    maxima, totals, accumulated = causal_block(
        empty_state(group, q_width),
        q_here,
        lax.all_gather(k_here, "ctx", axis=0, tiled=True),
        lax.all_gather(v_here, "ctx", axis=0, tiled=True),
        own_base,
    )
    finals = (
        (accumulated.reshape(group, -1, HEAD_WIDTH) / totals[..., None])
        .reshape(group, q_width)
        .astype(jnp.bfloat16)
    )
    return lax.all_to_all(finals, "head", split_axis=0, concat_axis=1, tiled=True)


def solution(mesh):
    in_specs = (P(("ctx", "head"), None), P(("ctx", "head"), None), P(("ctx", "head"), None))
    out_specs = P(("ctx", "head"), None)
    return jax.shard_map(
        per_device, mesh=mesh, in_specs=in_specs, out_specs=out_specs, check_vma=False
    )
```

profile of v0, /device:TPU:25, one launch (start us, length us, event | category | flops | bytes accessed | tf_op | source)
XLA Modules:
  0.0 387.3 jit_solution(15765268616346169088)
XLA Ops:
  7.9 25.4 %all_to_all.73 = bf16[128,32,128]{2,0,1:T(8,128)(2,1)} all-to-all(bf16[128,32,128]{2,0,1:T(8,128)(2,1)S(1)} %bitcast.137), channel_id=1, replica_groups=mesh['ctx'=4,'head'=32] {'head'}, dimensions={1} | all-to-all | bytes 2097152 | tf_op jit(solution)/shard_map/all_to_all | solution.py:113
  33.7 20.8 %all_to_all.74 = bf16[128,32,128]{2,0,1:T(8,128)(2,1)} all-to-all(bf16[128,32,128]{2,0,1:T(8,128)(2,1)S(1)} %bitcast.138), channel_id=1, replica_groups=mesh['ctx'=4,'head'=32] {'head'}, dimensions={1} | all-to-all | bytes 2097152 | tf_op jit(solution)/shard_map/all_to_all | solution.py:114
  55.8 4.0 %all-to-all-start = ((bf16[128,32,128]{2,0,1:T(8,128)(2,1)}), bf16[128,32,128]{2,0,1:T(8,128)(2,1)S(1)}, u32[]{:S(2)}, u32[]{:S(2)}) async-start(bf16[128,32,128]{2,0,1:T(8,128)(2,1)} %copy_bitcast_fusion), calls=%async_computation | async-start | bytes 2097152 | tf_op jit(solution)/shard_map/all_to_all | solution.py:112
  59.7 16.9 %all-to-all-done = bf16[128,32,128]{2,0,1:T(8,128)(2,1)S(1)} async-done(((bf16[128,32,128]{2,0,1:T(8,128)(2,1)}), bf16[128,32,128]{2,0,1:T(8,128)(2,1)S(1)}, u32[]{:S(2)}, u32[]{:S(2)}) %all-to-all-start) | async-done | bytes 1048608 | tf_op jit(solution)/shard_map/all_to_all | solution.py:112
  77.3 50.3 %all-gather.5.cloned.1.call-done = bf16[16384,128]{1,0:T(8,128)(2,1)} async-done(((bf16[4096,128]{1,0:T(8,128)(2,1)}), bf16[16384,128]{1,0:T(8,128)(2,1)}) %all-gather.5.cloned.1.call-update) | async-done | bytes 4194320 | tf_op jit(solution)/shard_map/all_gather | solution.py:123
  129.2 222.8 %while.92 = (s32[]{:T(128)}, f32[4096,1]{0,1:T(1,128)S(1)}, f32[4096,1]{0,1:T(1,128)S(1)}, f32[4096,128]{1,0:T(8,128)}, s32[]{:T(128)}, /*index=5*/bf16[4096,128...) while((s32[]{:T(128)}, f32[4096,1]{0,1:T(1,128)S(1)}, ...), condition=%wide.region_9.10_spmd, body=%wide.region_0.9_spmd.sunk | while | flops 553916416 | bytes 18215864 | solution.py:87
  130.3 48.3 %while.93 = (s32[]{:T(128)}, f32[1024,1]{0,1:T(1,128)S(1)}, f32[1024,1]{0,1:T(1,128)S(1)}, f32[1024,128]{1,0:T(8,128)S(1)}, s32[]{:T(128)}, /*index=5*/s32[]{:T(...) while((s32[]{:T(128)}, f32[1024,1]{0,1:T(1,128)S(1)}, ...), condition=%wide.region_8.8_spmd, body=%wide.region_1.7_spmd.sunk | while | flops 553916416 | bytes 15561081 | solution.py:79
  131.4 2.5 conditional.2
  135.0 2.5 conditional.2
  138.6 2.5 conditional.2
  142.2 2.5 conditional.2
  145.8 2.5 conditional.2
  149.4 2.5 conditional.2
  153.0 2.5 conditional.2
  156.6 2.5 conditional.2
  160.2 2.5 conditional.2
  163.9 2.5 conditional.2
  167.5 2.5 conditional.2
  171.1 2.5 conditional.2
  174.7 3.9 %conditional.2 = (f32[1024,1]{0,1:T(1,128)S(1)}, f32[1024,1]{0,1:T(1,128)S(1)}, f32[1024,128]{1,0:T(8,128)S(1)}) conditional(s32[]{:T(128)} %clamp.4, (bf16[1024,128]{1,0:T(8,128)(2,1)S(1)}, bf16[1024,128]{1,0:T(8,128)(2,1)S(1)}, f32[1024,1]{0,1:T(1,128)S(1)}, f32[1024,1]{0,1:T(1,128)S(1)}, f32[1024,128]{1,0:T(8,128)S(1)}, ...), branch_computations={%region_2.3_spmd, %region_5.6_spmd} | conditional | flops 553916416 | bytes 14512160 | solution.py:69
  180.6 51.9 %while.93 = (s32[]{:T(128)}, f32[1024,1]{0,1:T(1,128)S(1)}, f32[1024,1]{0,1:T(1,128)S(1)}, f32[1024,128]{1,0:T(8,128)S(1)}, s32[]{:T(128)}, /*index=5*/s32[]{:T(...) while((s32[]{:T(128)}, f32[1024,1]{0,1:T(1,128)S(1)}, ...), condition=%wide.region_8.8_spmd, body=%wide.region_1.7_spmd.sunk | while | flops 553916416 | bytes 15561081 | solution.py:79
  188.9 2.5 conditional.2
  192.5 2.5 conditional.2
  196.1 2.5 conditional.2
  199.7 2.5 conditional.2
  203.3 2.5 conditional.2
  206.9 2.5 conditional.2
  210.5 2.5 conditional.2
  214.1 2.5 conditional.2
  217.7 2.5 conditional.2
  221.4 2.5 conditional.2
  225.0 2.5 conditional.2
  228.6 3.9 %conditional.2 = (f32[1024,1]{0,1:T(1,128)S(1)}, f32[1024,1]{0,1:T(1,128)S(1)}, f32[1024,128]{1,0:T(8,128)S(1)}) conditional(s32[]{:T(128)} %clamp.4, (bf16[1024,128]{1,0:T(8,128)(2,1)S(1)}, bf16[1024,128]{1,0:T(8,128)(2,1)S(1)}, f32[1024,1]{0,1:T(1,128)S(1)}, f32[1024,1]{0,1:T(1,128)S(1)}, f32[1024,128]{1,0:T(8,128)S(1)}, ...), branch_computations={%region_2.3_spmd, %region_5.6_spmd} | conditional | flops 553916416 | bytes 14512160 | solution.py:69
  234.5 55.5 %while.93 = (s32[]{:T(128)}, f32[1024,1]{0,1:T(1,128)S(1)}, f32[1024,1]{0,1:T(1,128)S(1)}, f32[1024,128]{1,0:T(8,128)S(1)}, s32[]{:T(128)}, /*index=5*/s32[]{:T(...) while((s32[]{:T(128)}, f32[1024,1]{0,1:T(1,128)S(1)}, ...), condition=%wide.region_8.8_spmd, body=%wide.region_1.7_spmd.sunk | while | flops 553916416 | bytes 15561081 | solution.py:79
  242.8 2.5 conditional.2
  246.4 2.5 conditional.2
  250.0 2.5 conditional.2
  253.6 2.5 conditional.2
  286.1 3.9 %conditional.2 = (f32[1024,1]{0,1:T(1,128)S(1)}, f32[1024,1]{0,1:T(1,128)S(1)}, f32[1024,128]{1,0:T(8,128)S(1)}) conditional(s32[]{:T(128)} %clamp.4, (bf16[1024,128]{1,0:T(8,128)(2,1)S(1)}, bf16[1024,128]{1,0:T(8,128)(2,1)S(1)}, f32[1024,1]{0,1:T(1,128)S(1)}, f32[1024,1]{0,1:T(1,128)S(1)}, f32[1024,128]{1,0:T(8,128)S(1)}, ...), branch_computations={%region_2.3_spmd, %region_5.6_spmd} | conditional | flops 553916416 | bytes 14512160 | solution.py:69
  292.0 59.1 %while.93 = (s32[]{:T(128)}, f32[1024,1]{0,1:T(1,128)S(1)}, f32[1024,1]{0,1:T(1,128)S(1)}, f32[1024,128]{1,0:T(8,128)S(1)}, s32[]{:T(128)}, /*index=5*/s32[]{:T(...) while((s32[]{:T(128)}, f32[1024,1]{0,1:T(1,128)S(1)}, ...), condition=%wide.region_8.8_spmd, body=%wide.region_1.7_spmd.sunk | while | flops 553916416 | bytes 15561081 | solution.py:79
  293.1 2.5 conditional.2
  300.3 2.5 conditional.2
  307.5 2.5 conditional.2
  314.7 2.5 conditional.2
  321.9 2.5 conditional.2
  329.1 2.5 conditional.2
  347.2 3.9 %conditional.2 = (f32[1024,1]{0,1:T(1,128)S(1)}, f32[1024,1]{0,1:T(1,128)S(1)}, f32[1024,128]{1,0:T(8,128)S(1)}) conditional(s32[]{:T(128)} %clamp.4, (bf16[1024,128]{1,0:T(8,128)(2,1)S(1)}, bf16[1024,128]{1,0:T(8,128)(2,1)S(1)}, f32[1024,1]{0,1:T(1,128)S(1)}, f32[1024,1]{0,1:T(1,128)S(1)}, f32[1024,128]{1,0:T(8,128)S(1)}, ...), branch_computations={%region_2.3_spmd, %region_5.6_spmd} | conditional | flops 553916416 | bytes 14512160 | solution.py:69
  353.9 24.6 %all_to_all.75 = bf16[32,128,128]{2,1,0:T(8,128)(2,1)S(1)} all-to-all(bf16[32,128,128]{2,1,0:T(8,128)(2,1)S(1)} %bitcast.136), channel_id=1, replica_groups=mesh['ctx'=4,'head'=32] {'head'}, dimensions={0} | all-to-all | bytes 2097152 | tf_op jit(solution)/shard_map/all_to_all | solution.py:131
  (417 shorter events, 279.6 us)
Async XLA Ops:
  6.5 48.0 %copy-start = (bf16[128,4096]{1,0:T(8,128)(2,1)S(1)}, bf16[128,4096]{1,0:T(8,128)(2,1)}, u32[]{:S(2)}) copy-start(bf16[128,4096]{1,0:T(8,128)(2,1)} %param.9) | copy-start | bytes 3145732
  6.5 26.8 %copy-start.1 = (bf16[128,1024]{1,0:T(8,128)(2,1)S(1)}, bf16[128,1024]{1,0:T(8,128)(2,1)}, u32[]{:S(2)}) copy-start(bf16[128,1024]{1,0:T(8,128)(2,1)} %param.11) | copy-start | bytes 786436
  6.5 70.8 %all-gather.3.cloned.1.call-start = ((), (), s32[]{:S(2)}) async-start(), calls=%async_computation.4 | async-start | bytes 5242880 | tf_op jit(solution)/shard_map/all_gather | solution.py:122
  33.3 94.3 %all-gather.5.cloned.1.call-start = ((), (), s32[]{:S(2)}) async-start(), calls=%async_computation.5 | async-start | bytes 5242880 | tf_op jit(solution)/shard_map/all_gather | solution.py:123
  55.8 20.9 %all-to-all-start = ((bf16[128,32,128]{2,0,1:T(8,128)(2,1)}), bf16[128,32,128]{2,0,1:T(8,128)(2,1)S(1)}, u32[]{:S(2)}, u32[]{:S(2)}) async-start(bf16[128,32,128]{2,0,1:T(8,128)(2,1)} %copy_bitcast_fusion), calls=%async_computation | async-start | bytes 2097152 | tf_op jit(solution)/shard_map/all_to_all | solution.py:112
Sparse Core Ops, SparseCore 0:
  33.5 43.8 all-gather.2
  79.0 48.5 all-gather.4
where the time goes:
time: 389 us; the launch traced here: 387 us
  matrix products  100 us (26%)
  local copies, waits for them, and re-layouts  76.3 us (20%)
  blocking collectives  70.8 us (18%)
  waiting for transfers between devices  67.9 us (17%)
  other arithmetic  49.7 us (13%)
  between operations  13.5 us (3%)
  loops' own time  4.59 us (1%)
  starting transfers between devices  3.99 us (1%)
    dynamic_slice x58, local copies, waits for them, and re-layouts, over_keys(): lax.dynamic_slice_in_dim(v_block, key_index * key_tile, key_tile, 0)  62.1 us
    dot_general x58, matrix products, attend(): jnp.einsum('rkgt,tkd->rkgd', weights.astype(jnp.bfloat16), v_heads, prefe...  58.7 us
    all_gather x1, waiting for transfers between devices, per_device(): lax.all_gather(v_here, 'ctx', axis=0, tiled=True)  50.3 us
    reduce_sum x58, other arithmetic, attend(): jnp.sum(weights, axis=-1)  45.9 us
    dot_general x58, matrix products, attend(): jnp.einsum('rkgd,tkd->rkgt', q_heads, k_heads, preferred_element_type=jnp...  41.8 us
    all_to_all x1, blocking collectives, per_device(): lax.all_to_all(k_wide, 'head', split_axis=1, concat_axis=0, tiled=True)  25.4 us
    all_to_all x1, blocking collectives, per_device(): lax.all_to_all(finals, 'head', split_axis=0, concat_axis=1, tiled=True)  24.6 us
    all_to_all x1, blocking collectives, per_device(): lax.all_to_all(v_wide, 'head', split_axis=1, concat_axis=0, tiled=True)  20.8 us
  transfers between devices with their start and end apart: 3, of which 3 were waited for; matrix products, arithmetic and copies ran while one was open for 0% of the time, Pallas kernels for 0%

commit v1 on v0

v1 whole, which is shorter than its diff:
```python
import jax
import jax.numpy as jnp
from jax import lax
from jax.experimental import pallas as pl
from jax.experimental.pallas import tpu as pltpu
from jax.sharding import PartitionSpec as P

BLOCK = 128
WIDTH = 128
CHUNK = 1024
GROUP = 4 * WIDTH
SLOTS = 8
LOG2_SCALE = WIDTH**-0.5 * 1.4426950408889634
MESH = pl.DeviceIdType.MESH
F32 = jnp.float32
BF16 = jnp.bfloat16


def kernel(
    q_ref, k_ref, v_ref, out_ref,
    kv, vt, q_in, q_pair, peak, total, acc, score_a, score_b, o_buf,
    local_sem, home_send, home_recv, x_send, x_recv, z_send, z_recv, far_send, far_recv,
    core_send, core_recv, out_send, out_recv,
):
    y = lax.axis_index("ctx")
    head = lax.axis_index("head")
    x, zc = head // 8, lax.rem(head, 8)
    z, c = zc // 2, lax.rem(zc, 2)
    low = lax.min(x, 3 - x)
    x_mate = x + 1 - 2 * lax.rem(x, 2)
    z_up, z_down, z_far = lax.rem(z + 1, 4), lax.rem(z + 3, 4), lax.rem(z + 2, 4)
    my_slot = 2 * y + x // 2
    my_head = 2 * y + x // 2

    def at(ctx, x_, z_, c_):
        return (ctx, x_ * 8 + z_ * 2 + c_)

    homes = []
    for dy in range(4):
        for dx in range(2):
            homes.append((lax.rem(y + dy, 4), x if dx == 0 else 3 - x))
    mate, up, down, twin = at(y, x_mate, z, c), at(y, x, z_up, c), at(y, x, z_down, c), at(y, x, z, 1 - c)

    barrier = pltpu.get_barrier_semaphore()
    for hy, hx in homes[1:]:
        pl.semaphore_signal(barrier, inc=1, device_id=at(hy, hx, z, c), device_id_type=MESH)
    for other in (mate, up, down, twin):
        pl.semaphore_signal(barrier, inc=1, device_id=other, device_id_type=MESH)
    pl.semaphore_wait(barrier, 11)

    home, along_x, along_z = (home_send, home_recv), (x_send, x_recv), (z_send, z_recv)
    far, core = (far_send, far_recv), (core_send, core_recv)
    sent = []

    def send(src, dst, sems, index, device, recv_index=None):
        send_sem, recv_sem = sems
        pltpu.make_async_remote_copy(
            src_ref=src,
            dst_ref=dst,
            send_sem=send_sem.at[index],
            recv_sem=recv_sem.at[index if recv_index is None else recv_index],
            device_id=device,
            device_id_type=MESH,
        ).start()
        sent.append((send_sem, index, src.shape))

    def arrived(dst, recv_sem):
        pltpu.make_async_remote_copy(
            src_ref=dst, dst_ref=dst, send_sem=local_sem.at[0], recv_sem=recv_sem, device_id=mate, device_id_type=MESH
        ).wait_recv()

    my_chunk = 4 * y + x

    def columns(head_, width):
        return pl.ds(pl.multiple_of(head_ * width, width), width)

    own = [
        pltpu.make_async_copy(k_ref.at[:, columns(my_head, WIDTH)], kv.at[my_chunk, zc, 0], local_sem.at[0]),
        pltpu.make_async_copy(v_ref.at[:, columns(my_head, WIDTH)], kv.at[my_chunk, zc, 1], local_sem.at[1]),
        pltpu.make_async_copy(q_ref.at[:, columns(my_head, GROUP)], q_in.at[my_slot], local_sem.at[2]),
    ]
    for copy in own:
        copy.start()
    for i, (hy, hx) in enumerate(homes):
        if i:
            there, to = 2 * hy + hx // 2, at(hy, hx, z, c)
            send(k_ref.at[:, columns(there, WIDTH)], kv.at[my_chunk, zc, 0], home, (0, i), to, (0, my_slot))
            send(v_ref.at[:, columns(there, WIDTH)], kv.at[my_chunk, zc, 1], home, (1, i), to, (1, my_slot))
    for i, (hy, hx) in enumerate(homes):
        if i:
            there, to = 2 * hy + hx // 2, at(hy, hx, z, c)
            send(q_ref.at[:, columns(there, GROUP)], q_in.at[my_slot], home, (2, i), to, (2, my_slot))

    peak[...] = jnp.full_like(peak, -1e30)
    total[...] = jnp.zeros_like(total)
    acc[...] = jnp.zeros_like(acc)
    for copy in own:
        copy.wait()

    def own_chunk(quarter, i):
        return 4 * quarter + (low if i == 0 else 3 - low)

    mate_low = 1 - low

    def mate_chunk(quarter, i):
        return 4 * quarter + (mate_low if i == 0 else 3 - mate_low)

    def rows(quarter, z_):
        return kv.at[pl.ds(4 * quarter, 4), 2 * z_ + c]

    def gather_1(quarter):
        for i in range(2):
            slot = 2 * quarter + i

            @pl.when(slot != my_slot)
            def _():
                arrived(kv.at[own_chunk(quarter, i), zc, 0], home_recv.at[0, slot])
                arrived(kv.at[own_chunk(quarter, i), zc, 1], home_recv.at[1, slot])

        for i in range(2):
            block = kv.at[own_chunk(quarter, i), zc]
            send(block, block, along_x, (quarter, i), mate)
            send(block, block, along_z, (quarter, 0, i), up)
            send(block, block, along_z, (quarter, 1, i), down)

    def gather_2(quarter):
        for i in range(2):
            block = kv.at[mate_chunk(quarter, i), zc]
            arrived(block, x_recv.at[quarter, i])
            send(block, block, along_z, (quarter, 0, 2 + i), up)
            send(block, block, along_z, (quarter, 1, 2 + i), down)
        send(rows(quarter, z), rows(quarter, z), core, (quarter, 0), twin)

    def gather_3(quarter):
        for way, z_ in ((0, z_down), (1, z_up)):
            for i in range(2):
                arrived(kv.at[own_chunk(quarter, i), 2 * z_ + c], z_recv.at[quarter, way, i])
                arrived(kv.at[mate_chunk(quarter, i), 2 * z_ + c], z_recv.at[quarter, way, 2 + i])
            half = kv.at[pl.ds(4 * quarter, 4), 2 * z_ + c, way]
            send(half, half, far, (quarter, way), up if way == 0 else down)
            send(rows(quarter, z_), rows(quarter, z_), core, (quarter, 1 + way), twin)

    def gather_4(quarter):
        for way in range(2):
            arrived(kv.at[pl.ds(4 * quarter, 4), 2 * z_far + c, way], far_recv.at[quarter, way])
        send(rows(quarter, z_far), rows(quarter, z_far), core, (quarter, 3), twin)

    def gather_5(quarter):
        for i, z_ in enumerate((z, z_down, z_up, z_far)):
            arrived(kv.at[pl.ds(4 * quarter, 4), 2 * z_ + 1 - c], core_recv.at[quarter, i])

    def turn_values(quarter):
        def one(i, _):
            chunk = 4 * quarter + i
            for b in range(8):
                vt[chunk, :, b * BLOCK : (b + 1) * BLOCK] = kv[chunk, b, 1].T
            return 0

        lax.fori_loop(0, 4, one, 0)

    def split_queries(slot):
        for h in range(4):
            scaled = q_in[slot, :, h * WIDTH : (h + 1) * WIDTH].astype(F32) * LOG2_SCALE
            top = scaled.astype(BF16)
            q_pair[slot, h * BLOCK : (h + 1) * BLOCK, :WIDTH] = top
            q_pair[slot, h * BLOCK : (h + 1) * BLOCK, WIDTH:] = (scaled - top.astype(F32)).astype(BF16)

    def score(where, dst):
        slot, chunk = where
        k = kv[chunk, :, 0].reshape(CHUNK, WIDTH)
        dst[...] = lax.dot_general(
            jnp.concatenate([k, k], axis=1), q_pair[slot], (((1,), (1,)), ((), ())), preferred_element_type=F32
        )

    def absorb(where, src, masked=False):
        slot, chunk = where
        s = src[...]
        if masked:
            key = lax.broadcasted_iota(jnp.int32, s.shape, 0)
            token = lax.rem(lax.broadcasted_iota(jnp.int32, s.shape, 1), BLOCK)
            s = jnp.where(key <= token + zc * BLOCK, s, -1e30)
        old = peak[slot]
        new = jnp.maximum(old, jnp.max(s, axis=0, keepdims=True))
        weights = jnp.exp2(s - new)
        rescale = jnp.exp2(old - new)
        peak[slot] = new
        total[slot] = total[slot] * rescale + jnp.sum(weights, axis=0, keepdims=True)
        acc[slot] = acc[slot] * rescale + jnp.dot(vt[chunk], weights.astype(BF16), preferred_element_type=F32)

    def finish(slot, i):
        y_, x_ = slot // 2, (low if i == 0 else 3 - low)
        for h in range(4):
            part = acc[slot, :, h * BLOCK : (h + 1) * BLOCK] / total[slot, :, h * BLOCK : (h + 1) * BLOCK]
            o_buf[slot, :, h * WIDTH : (h + 1) * WIDTH] = part.T.astype(BF16)

        @pl.when(slot != my_slot)
        def _():
            pltpu.make_async_remote_copy(
                src_ref=o_buf.at[slot],
                dst_ref=out_ref.at[:, columns(my_head, GROUP)],
                send_sem=out_send.at[slot],
                recv_sem=out_recv.at[my_head],
                device_id=at(y_, x_, z, c),
                device_id_type=MESH,
            ).start()

        @pl.when(slot == my_slot)
        def _():
            pltpu.make_async_copy(o_buf.at[slot], out_ref.at[:, columns(my_head, GROUP)], local_sem.at[3]).start()

    gather_1(0)
    gather_2(0)
    gather_1(1)
    gather_3(0)
    gather_2(1)
    gather_4(0)
    gather_5(0)
    for slot in range(SLOTS):

        @pl.when(slot != my_slot)
        def _():
            arrived(q_in.at[slot], home_recv.at[2, slot])

        split_queries(slot)

    def both(one, quarter, other, earlier):
        one(quarter)
        other(earlier)

    steps = {
        (0, 1): lambda: gather_3(1),
        (0, 2): lambda: gather_1(2),
        (0, 4): lambda: both(gather_2, 2, gather_4, 1),
        (0, 6): lambda: gather_3(2),
        (0, 7): lambda: gather_1(3),
        (0, 9): lambda: both(gather_2, 3, gather_4, 2),
        (0, 12): lambda: gather_3(3),
        (1, 3): lambda: gather_4(3),
    }

    for p in range(4):
        if p:
            gather_5(p)
        turn_values(p)
        wide = 8 * (3 - p)

        def unit(u, p=p, wide=wide):
            i = u - wide
            second = jnp.where(i >= low, 1, 0)
            slot = jnp.where(u < wide, 2 * (p + 1) + u // 4, 2 * p + second)
            chunk = 4 * p + jnp.where(u < wide, lax.rem(u, 4), i - second * low)
            return slot, chunk

        score(unit(jnp.int32(0)), score_a)

        def pair(i, _, p=p, unit=unit):
            for (phase, step), action in steps.items():
                if phase == p:
                    pl.when(i == step)(action)
            score(unit(2 * i + 1), score_b)
            absorb(unit(2 * i), score_a)
            score(unit(2 * i + 2), score_a)
            absorb(unit(2 * i + 1), score_b)
            return 0

        pairs = (wide + 2) // 2
        lax.fori_loop(0, pairs, pair, 0)
        first, second = (2 * p, 4 * p + low), (2 * p + 1, 4 * p + 3 - low)
        score(first, score_b)
        absorb(unit(jnp.int32(2 * pairs)), score_a)
        score(second, score_a)
        absorb(first, score_b, True)
        finish(2 * p, 0)
        absorb(second, score_a, True)
        finish(2 * p + 1, 1)

    for send_sem, index, shape in sent:
        held = {2: kv.at[0, 0, 0], 3: kv.at[0, 0], 4: kv.at[pl.ds(0, 4), 0]}[len(shape)]
        if shape == (4, BLOCK, WIDTH):
            held = kv.at[pl.ds(0, 4), 0, 0]
        elif shape == (BLOCK, GROUP):
            held = q_in.at[0]
        pltpu.make_async_remote_copy(
            src_ref=held, dst_ref=held, send_sem=send_sem.at[index], recv_sem=local_sem.at[0], device_id=mate,
            device_id_type=MESH,
        ).wait_send()
    for slot in range(SLOTS):
        y_, x_ = slot // 2, (low if slot % 2 == 0 else 3 - low)

        @pl.when(slot != my_slot)
        def _():
            piece = out_ref.at[:, pl.ds(slot * GROUP, GROUP)]
            done = pltpu.make_async_remote_copy(
                src_ref=o_buf.at[slot],
                dst_ref=piece,
                send_sem=out_send.at[slot],
                recv_sem=out_recv.at[slot],
                device_id=at(y_, x_, z, c),
                device_id_type=MESH,
            )
            done.wait_send()
            done.wait_recv()

        @pl.when(slot == my_slot)
        def _():
            pltpu.make_async_copy(o_buf.at[slot], out_ref.at[:, columns(my_head, GROUP)], local_sem.at[3]).wait()


def per_device(queries, keys, values):
    sem = pltpu.SemaphoreType.DMA
    return pl.pallas_call(
        kernel,
        out_shape=jax.ShapeDtypeStruct(queries.shape, BF16),
        in_specs=[pl.BlockSpec(memory_space=pl.ANY)] * 3,
        out_specs=pl.BlockSpec(memory_space=pl.ANY),
        scratch_shapes=[
            pltpu.VMEM((16, 8, 2, BLOCK, WIDTH), BF16),
            pltpu.VMEM((16, WIDTH, CHUNK), BF16),
            pltpu.VMEM((SLOTS, BLOCK, GROUP), BF16),
            pltpu.VMEM((SLOTS, 4 * BLOCK, 2 * WIDTH), BF16),
            pltpu.VMEM((SLOTS, 1, 4 * BLOCK), F32),
            pltpu.VMEM((SLOTS, 1, 4 * BLOCK), F32),
            pltpu.VMEM((SLOTS, WIDTH, 4 * BLOCK), F32),
            pltpu.VMEM((CHUNK, 4 * BLOCK), F32),
            pltpu.VMEM((CHUNK, 4 * BLOCK), F32),
            pltpu.VMEM((SLOTS, BLOCK, GROUP), BF16),
            sem((4,)),
            sem((3, 8)), sem((3, 8)),
            sem((4, 2)), sem((4, 2)),
            sem((4, 2, 4)), sem((4, 2, 4)),
            sem((4, 2)), sem((4, 2)),
            sem((4, 4)), sem((4, 4)),
            sem((8,)), sem((8,)),
        ],
        compiler_params=pltpu.CompilerParams(
            collective_id=0, has_side_effects=True, vmem_limit_bytes=56 * 2**20
        ),
        name="causal_attention",
    )(queries, keys, values)


def solution(mesh):
    spec = P(("ctx", "head"), None)
    return jax.shard_map(per_device, mesh=mesh, in_specs=(spec, spec, spec), out_specs=spec, check_vma=False)
```

time: 389 us -> 98.9 us (0.25)
  matrix products: 100 us -> 0 us
  Pallas kernels: 0 us -> 94.9 us
  local copies, waits for them, and re-layouts: 76.3 us -> 2.29 us
  blocking collectives: 70.8 us -> 0 us
  waiting for transfers between devices: 67.9 us -> 0 us
  other arithmetic: 49.7 us -> 0 us
  between operations: 13.5 us -> 0.01 us
  loops' own time: 4.59 us -> 0 us
  starting transfers between devices: 3.99 us -> 0 us
    dot_general x116 -> x0, matrix products: 100 us -> none  [the longest x58 58.7 us: attend(): jnp.einsum('rkgt,tkd->rkgd', weights.astype(jnp.bfloat16), v_heads, prefe...]
    pallas_call x0 -> x1, Pallas kernels: none -> 94.9 us  [per_device(): pl.pallas_call(kernel, out_shape=jax.ShapeDtypeStruct(queries.shape, BF16...]
    all_to_all x3 -> x0, blocking collectives: 70.8 us -> none  [the longest x1 25.4 us: per_device(): lax.all_to_all(k_wide, 'head', split_axis=1, concat_axis=0, tiled=True)]
    dynamic_slice x74 -> x0, local copies, waits for them, and re-layouts: 66.5 us -> none  [the longest x58 62.1 us: over_keys(): lax.dynamic_slice_in_dim(v_block, key_index * key_tile, key_tile, 0)]
    all_gather x2 -> x0, waiting for transfers between devices: 51 us -> none  [the longest x1 50.3 us: per_device(): lax.all_gather(v_here, 'ctx', axis=0, tiled=True)]
    reduce_sum x58 -> x0, other arithmetic: 45.9 us -> none  [attend(): jnp.sum(weights, axis=-1)]
    all_to_all x1 -> x0, waiting for transfers between devices: 16.9 us -> none  [per_device(): lax.all_to_all(queries, 'head', split_axis=1, concat_axis=0, tiled=True)]
    another operation x63 -> x0, loops' own time: 4.59 us -> none  [the longest x4 2.46 us: over_queries(): section = lax.fori_loop(jnp.int32(0), needed, over_keys, section)]
  transfers between devices with their start and end apart: 3 -> 0, of which waited for: 3 -> 0; matrix products, arithmetic and copies ran while one was open for 0% -> 0% of each run, Pallas kernels for 0% -> 0%
where the time goes in v1:
time: 98.9 us; the launch traced here: 97.2 us
  Pallas kernels  94.9 us (96%)
  local copies, waits for them, and re-layouts  2.29 us (2%)
    pallas_call x1, Pallas kernels, per_device(): pl.pallas_call(kernel, out_shape=jax.ShapeDtypeStruct(queries.shape, BF16...  94.9 us
    unnamed x1, local copies, waits for them, and re-layouts  2.29 us

profile of v1, /device:TPU:25, one launch (start us, length us, event | category | flops | bytes accessed | tf_op | source)
XLA Modules:
  0.0 97.2 jit_solution(17688644810754548357)
XLA Ops:
  0.0 94.9 %causal_attention.1 = bf16[128,4096]{1,0:T(8,128)(2,1)} custom-call(bf16[128,4096]{1,0:T(8,128)(2,1)} %q_ref.1, bf16[128,1024]{1,0:T(8,128)(2,1)} %k_ref.1, bf16[128,1024]{1,0:T(8,128)(2,1)} %v_ref.1), custom_call_target="tpu_custom_call" | custom-call | tf_op jit(solution)/shard_map/causal_attention/pallas_call | solution.py:311
  94.9 2.3 %copy.5 = bf16[128,4096]{1,0:T(8,128)(2,1)} copy(bf16[128,4096]{1,0:T(8,128)(2,1)} %causal_attention.1) | data formatting | bytes 2097152

commit v2 on v1

v2 whole, which is shorter than its diff:
```python
import jax
import jax.numpy as jnp
from jax import lax
from jax.experimental import pallas as pl
from jax.experimental.pallas import tpu as pltpu
from jax.sharding import PartitionSpec as P

BLOCK = 128
WIDTH = 128
GROUP = 4 * WIDTH
ROWS = 4 * BLOCK
CHUNK = 1024
PART = 2048
SPAN = 256
SLOTS = 8
UNITS = 28
LOG2_SCALE = WIDTH**-0.5 * 1.4426950408889634
MESH = pl.DeviceIdType.MESH
F32 = jnp.float32
BF16 = jnp.bfloat16


def kernel(
    q_ref, k_ref, v_ref, out_ref,
    kv, v_raw, v_turned, q_in, q_pair, peak, total, acc, score_a, score_b, top_a, top_b, o_buf,
    local_sem, home_send, home_recv, x_send, x_recv, z_send, z_recv, far_send, far_recv,
    core_send, core_recv, out_send, out_recv,
):
    y = lax.axis_index("ctx")
    head = lax.axis_index("head")
    x, zc = head // 8, lax.rem(head, 8)
    z, c = zc // 2, lax.rem(zc, 2)
    low = lax.min(x, 3 - x)
    half = x // 2
    x_mate = x + 1 - 2 * lax.rem(x, 2)
    z_up, z_down, z_far = lax.rem(z + 1, 4), lax.rem(z + 3, 4), lax.rem(z + 2, 4)
    my_slot = 2 * y + half
    my_head = 2 * y + half

    def at(ctx, x_, z_, c_):
        return (ctx, x_ * 8 + z_ * 2 + c_)

    homes = []
    for dy in (2, 1, 3, 0):
        for dx in (1, 0):
            homes.append((lax.rem(y + dy, 4), x if dx == 0 else 3 - x))
    homes = homes[:-1]
    mate, up, down, twin = at(y, x_mate, z, c), at(y, x, z_up, c), at(y, x, z_down, c), at(y, x, z, 1 - c)

    barrier = pltpu.get_barrier_semaphore()
    for hy, hx in homes:
        pl.semaphore_signal(barrier, inc=1, device_id=at(hy, hx, z, c), device_id_type=MESH)
    for other in (mate, up, down, twin):
        pl.semaphore_signal(barrier, inc=1, device_id=other, device_id_type=MESH)

    def columns(head_, width):
        return pl.ds(pl.multiple_of(head_ * width, width), width)

    my_chunk = 4 * y + half
    load_v = pltpu.make_async_copy(v_ref, v_raw, local_sem.at[0])
    load_v.start()
    own = [
        pltpu.make_async_copy(k_ref.at[:, columns(my_head, WIDTH)], kv.at[my_chunk, zc, 0], local_sem.at[1]),
        pltpu.make_async_copy(q_ref.at[:, columns(my_head, GROUP)], q_in.at[my_slot], local_sem.at[2]),
    ]
    for copy in own:
        copy.start()
    peak[...] = jnp.full_like(peak, -1e30)
    total[...] = jnp.zeros_like(total)
    acc[...] = jnp.zeros_like(acc)
    load_v.wait()
    for h in range(8):
        v_turned[h] = v_raw[:, h * WIDTH : (h + 1) * WIDTH].T
    own.append(pltpu.make_async_copy(v_turned.at[my_head], kv.at[my_chunk, zc, 1], local_sem.at[3]))
    own[-1].start()

    pl.semaphore_wait(barrier, 11)

    home, along_x, along_z = (home_send, home_recv), (x_send, x_recv), (z_send, z_recv)
    far, core = (far_send, far_recv), (core_send, core_recv)
    sent = []

    def send(src, dst, sems, index, device, recv_index=None):
        send_sem, recv_sem = sems
        pltpu.make_async_remote_copy(
            src_ref=src,
            dst_ref=dst,
            send_sem=send_sem.at[index],
            recv_sem=recv_sem.at[index if recv_index is None else recv_index],
            device_id=device,
            device_id_type=MESH,
        ).start()
        sent.append((send_sem, index, src.shape))

    def arrived(dst, recv_sem):
        pltpu.make_async_remote_copy(
            src_ref=dst, dst_ref=dst, send_sem=local_sem.at[0], recv_sem=recv_sem, device_id=mate, device_id_type=MESH
        ).wait_recv()

    for i, (hy, hx) in enumerate(homes):
        there, to = 2 * hy + hx // 2, at(hy, hx, z, c)
        send(k_ref.at[:, columns(there, WIDTH)], kv.at[my_chunk, zc, 0], home, (0, i), to, (0, my_slot))
        send(v_turned.at[there], kv.at[my_chunk, zc, 1], home, (1, i), to, (1, my_slot))
    for i, (hy, hx) in enumerate(homes):
        there, to = 2 * hy + hx // 2, at(hy, hx, z, c)
        send(q_ref.at[:, columns(there, GROUP)], q_in.at[my_slot], home, (2, i), to, (2, my_slot))

    for copy in own:
        copy.wait()

    def pair(quarter, m, z_, c_=c):
        return kv.at[pl.ds(4 * quarter + 2 * m, 2), 2 * z_ + c_]

    def half_pair(quarter, m, z_, way):
        return kv.at[pl.ds(4 * quarter + 2 * m, 2), 2 * z_ + c, way]

    def to_mate(quarter):
        for i in range(2):
            slot = 2 * quarter + i

            @pl.when(slot != my_slot)
            def _():
                arrived(kv.at[4 * quarter + i, zc, 0], home_recv.at[0, slot])
                arrived(kv.at[4 * quarter + i, zc, 1], home_recv.at[1, slot])

        send(pair(quarter, 0, z), pair(quarter, 1, z), along_x, (quarter,), mate)
        send(pair(quarter, 0, z), pair(quarter, 0, z), core, (quarter, 0, 0), twin)

    def to_ring(quarter, m):
        if m:
            arrived(pair(quarter, 1, z), x_recv.at[quarter])
            send(pair(quarter, 1, z), pair(quarter, 1, z), core, (quarter, 1, 0), twin)
        send(pair(quarter, m, z), pair(quarter, m, z), along_z, (quarter, m, 0), up)
        send(pair(quarter, m, z), pair(quarter, m, z), along_z, (quarter, m, 1), down)

    def round_ring(quarter, m):
        for way, z_ in ((0, z_down), (1, z_up)):
            arrived(pair(quarter, m, z_), z_recv.at[quarter, m, way])
            part = half_pair(quarter, m, z_, way)
            send(part, part, far, (quarter, m, way), up if way == 0 else down)
            send(pair(quarter, m, z_), pair(quarter, m, z_), core, (quarter, m, 1 + way), twin)

    def from_far(quarter, m):
        for way in range(2):
            arrived(half_pair(quarter, m, z_far, way), far_recv.at[quarter, m, way])
        send(pair(quarter, m, z_far), pair(quarter, m, z_far), core, (quarter, m, 3), twin)

    def from_twin(quarter, m):
        for i, z_ in enumerate((z, z_down, z_up, z_far)):
            arrived(pair(quarter, m, z_, 1 - c), core_recv.at[quarter, m, i])

    def split_queries(slot):
        @pl.when(slot != my_slot)
        def _():
            arrived(q_in.at[slot], home_recv.at[2, slot])

        for h in range(4):
            scaled = q_in[slot, :, h * WIDTH : (h + 1) * WIDTH].astype(F32) * LOG2_SCALE
            first = scaled.astype(BF16)
            q_pair[slot, h * BLOCK : (h + 1) * BLOCK, :WIDTH] = first
            q_pair[slot, h * BLOCK : (h + 1) * BLOCK, WIDTH:] = (scaled - first.astype(F32)).astype(BF16)

    def parts(chunks):
        blocks = [(chunk, b) for chunk in chunks for b in range(8)]
        return [blocks[i : i + PART // BLOCK] for i in range(0, len(blocks), PART // BLOCK)]

    def work(ahead, behind):
        ahead_parts = parts(ahead[1]) if ahead else []
        behind_parts = parts(behind[1]) if behind else []
        for start in range(0, ROWS, SPAN):
            columns_ = slice(start, start + SPAN)
            if behind:
                slot, _, src, src_top = behind
                old = peak[slot, :, columns_]
                new = jnp.maximum(old, jnp.max(src_top[:, columns_], axis=0, keepdims=True))
                rescale = jnp.exp2(old - new)
                peak[slot, :, columns_] = new
                sums, mixture = total[slot, :, columns_] * rescale, None
            highest = None
            for i in range(max(len(ahead_parts), len(behind_parts))):
                if i < len(ahead_parts):
                    slot_, chunks_, dst, dst_top, masked = ahead
                    k = jnp.concatenate([kv[chunk, b, 0] for chunk, b in ahead_parts[i]], axis=0)
                    rows = slice(i * PART, i * PART + k.shape[0])
                    s = lax.dot_general(
                        jnp.concatenate([k, k], axis=1), q_pair[slot_, columns_], (((1,), (1,)), ((), ())),
                        preferred_element_type=F32,
                    )
                    if masked and rows.stop > CHUNK * (len(chunks_) - 1):
                        past = rows.start - CHUNK * (len(chunks_) - 1)
                        key = past + lax.broadcasted_iota(jnp.int32, s.shape, 0)
                        token = lax.rem(lax.broadcasted_iota(jnp.int32, s.shape, 1), BLOCK)
                        s = jnp.where(key <= token + zc * BLOCK, s, -1e30)
                    dst[rows, columns_] = s
                    best = jnp.max(s.reshape(-1, 8, SPAN), axis=0)
                    highest = best if highest is None else jnp.maximum(highest, best)
                if i < len(behind_parts):
                    rows = slice(i * PART, i * PART + BLOCK * len(behind_parts[i]))
                    weights = jnp.exp2(src[rows, columns_] - new)
                    sums = sums + jnp.sum(weights.reshape(-1, 8, SPAN), axis=0)
                    v = jnp.concatenate([kv[chunk, b, 1] for chunk, b in behind_parts[i]], axis=1)
                    term = jnp.dot(v, weights.astype(BF16), preferred_element_type=F32)
                    mixture = term if mixture is None else mixture + term
            if ahead:
                dst_top[:, columns_] = highest
            if behind:
                total[slot, :, columns_] = sums
                acc[slot, :, columns_] = acc[slot, :, columns_] * rescale + mixture

    def finish(slot):
        for h in range(4):
            columns_ = slice(h * BLOCK, (h + 1) * BLOCK)
            part = acc[slot, :, columns_] / jnp.sum(total[slot, :, columns_], axis=0, keepdims=True)
            o_buf[slot, :, h * WIDTH : (h + 1) * WIDTH] = part.T.astype(BF16)

        @pl.when(slot != my_slot)
        def _():
            pltpu.make_async_remote_copy(
                src_ref=o_buf.at[slot],
                dst_ref=out_ref.at[:, columns(my_head, GROUP)],
                send_sem=out_send.at[slot],
                recv_sem=out_recv.at[my_head],
                device_id=at(slot // 2, low + lax.rem(slot, 2) * (3 - 2 * low), z, c),
                device_id_type=MESH,
            ).start()

        @pl.when(slot == my_slot)
        def _():
            pltpu.make_async_copy(o_buf.at[slot], out_ref.at[:, columns(my_head, GROUP)], local_sem.at[0]).start()

    to_mate(0)
    to_ring(0, 0)
    to_mate(1)
    to_mate(2)
    to_mate(3)
    round_ring(0, 0)
    to_ring(0, 1)
    from_far(0, 0)
    to_ring(1, 0)
    for slot in range(SLOTS):
        split_queries(slot)
    from_twin(0, 0)

    def unit(u):
        p = jnp.where(u >= 13, 1, 0) + jnp.where(u >= 22, 1, 0) + jnp.where(u >= 27, 1, 0)
        i = u - (13 * p - 2 * p * (p - 1))
        later = 2 * (3 - p)
        kind = jnp.where(i >= later, 1, 0) + jnp.where(i >= 2 * later, 1, 0)
        slot = jnp.where(kind == 2, 2 * p + 1, 2 * (p + 1) + i - kind * later)
        one = 4 * p + 2 * lax.rem(kind, 2)
        return slot, (one, one + 1 + lax.div(kind, 2))

    steps = {
        0: [(round_ring, 0, 1)],
        1: [(round_ring, 1, 0), (to_ring, 1, 1)],
        2: [(from_far, 0, 1), (from_twin, 0, 1)],
        3: [(to_ring, 2, 0), (from_far, 1, 0)],
        4: [(round_ring, 1, 1), (to_ring, 2, 1)],
        5: [(round_ring, 2, 0), (from_far, 1, 1), (to_ring, 3, 0)],
        6: [(from_twin, 1, 0), (round_ring, 2, 1), (to_ring, 3, 1)],
        7: [(from_far, 2, 0), (from_twin, 1, 1)],
        8: [(round_ring, 3, 0), (from_far, 2, 1)],
        9: [(round_ring, 3, 1)],
        10: [(from_far, 3, 0), (from_twin, 2, 0)],
        11: [(from_far, 3, 1), (from_twin, 2, 1)],
        12: [(from_twin, 3, 0), (from_twin, 3, 1)],
    }

    def do(actions):
        def run():
            for action, quarter, m in actions:
                action(quarter, m)

        return run

    def ahead_of(u, dst, dst_top):
        return (*unit(u), dst, dst_top, False)

    def behind_of(u, src, src_top):
        return (*unit(u), src, src_top)

    work(ahead_of(jnp.int32(0), score_a, top_a), None)

    def full(i, _):
        for step, actions in steps.items():
            pl.when(i == step)(do(actions))
        work(ahead_of(2 * i + 1, score_b, top_b), behind_of(2 * i, score_a, top_a))
        work(ahead_of(lax.min(2 * i + 2, UNITS - 1), score_a, top_a), behind_of(2 * i + 1, score_b, top_b))
        return 0

    lax.fori_loop(0, UNITS // 2, full, 0)

    def quarter_of(k):
        return lax.rem(y + k + 1 + jnp.where(k == 0, 1, 0) - jnp.where(k == 1, 1, 0), 4)

    def wide(k):
        p = quarter_of(k)
        return 2 * p + 1 - low, (4 * p + 3 - low, 4 * p + 1 - low)

    def narrow(k):
        p = quarter_of(k)
        return 2 * p + low, (4 * p + low,)

    for where in (wide, narrow):
        work((*where(jnp.int32(0)), score_a, top_a, True), None)

        def edge(k, _, where=where):
            one, two = where(2 * k), where(2 * k + 1)
            work((*two, score_b, top_b, True), (*one, score_a, top_a))
            finish(one[0])
            work((*where(lax.min(2 * k + 2, 3)), score_a, top_a, True), (*two, score_b, top_b))
            finish(two[0])
            return 0

        lax.fori_loop(0, 2, edge, 0)

    for send_sem, index, shape in sent:
        held = {
            (BLOCK, WIDTH): kv.at[0, 0, 0],
            (BLOCK, GROUP): q_in.at[0],
            (2, 2, BLOCK, WIDTH): kv.at[pl.ds(0, 2), 0],
            (2, BLOCK, WIDTH): kv.at[pl.ds(0, 2), 0, 0],
        }[shape]
        pltpu.make_async_remote_copy(
            src_ref=held, dst_ref=held, send_sem=send_sem.at[index], recv_sem=local_sem.at[0], device_id=mate,
            device_id_type=MESH,
        ).wait_send()
    for slot in range(SLOTS):

        @pl.when(slot != my_slot)
        def _():
            done = pltpu.make_async_remote_copy(
                src_ref=o_buf.at[slot],
                dst_ref=out_ref.at[:, pl.ds(slot * GROUP, GROUP)],
                send_sem=out_send.at[slot],
                recv_sem=out_recv.at[slot],
                device_id=mate,
                device_id_type=MESH,
            )
            done.wait_send()
            done.wait_recv()

        @pl.when(slot == my_slot)
        def _():
            pltpu.make_async_copy(o_buf.at[slot], out_ref.at[:, columns(my_head, GROUP)], local_sem.at[0]).wait()


def per_device(queries, keys, values):
    sem = pltpu.SemaphoreType.DMA
    return pl.pallas_call(
        kernel,
        out_shape=jax.ShapeDtypeStruct(queries.shape, BF16),
        in_specs=[pl.BlockSpec(memory_space=pl.ANY)] * 3,
        out_specs=pl.BlockSpec(memory_space=pl.ANY),
        scratch_shapes=[
            pltpu.VMEM((16, 8, 2, BLOCK, WIDTH), BF16),
            pltpu.VMEM((BLOCK, 8 * WIDTH), BF16),
            pltpu.VMEM((8, WIDTH, BLOCK), BF16),
            pltpu.VMEM((SLOTS, BLOCK, GROUP), BF16),
            pltpu.VMEM((SLOTS, ROWS, 2 * WIDTH), BF16),
            pltpu.VMEM((SLOTS, 1, ROWS), F32),
            pltpu.VMEM((SLOTS, 8, ROWS), F32),
            pltpu.VMEM((SLOTS, WIDTH, ROWS), F32),
            pltpu.VMEM((2 * CHUNK, ROWS), F32),
            pltpu.VMEM((2 * CHUNK, ROWS), F32),
            pltpu.VMEM((8, ROWS), F32),
            pltpu.VMEM((8, ROWS), F32),
            pltpu.VMEM((SLOTS, BLOCK, GROUP), BF16),
            sem((4,)),
            sem((3, 7)), sem((3, 8)),
            sem((4,)), sem((4,)),
            sem((4, 2, 2)), sem((4, 2, 2)),
            sem((4, 2, 2)), sem((4, 2, 2)),
            sem((4, 2, 4)), sem((4, 2, 4)),
            sem((8,)), sem((8,)),
        ],
        compiler_params=pltpu.CompilerParams(
            collective_id=0, has_side_effects=True, vmem_limit_bytes=56 * 2**20
        ),
        name="causal_attention",
    )(queries, keys, values)


def solution(mesh):
    spec = P(("ctx", "head"), None)
    return jax.shard_map(per_device, mesh=mesh, in_specs=(spec, spec, spec), out_specs=spec, check_vma=False)
```

time: 98.9 us -> 92.6 us (0.936); the launches traced: 97.2 us -> 92.4 us
  Pallas kernels: 94.9 us -> 90.1 us
    pallas_call x1, Pallas kernels: 94.9 us -> 90.1 us  [per_device(): pl.pallas_call(kernel, out_shape=jax.ShapeDtypeStruct(queries.shape, BF16...]
where the time goes in v2:
time: 92.6 us; the launch traced here: 92.4 us
  Pallas kernels  90.1 us (97%)
  local copies, waits for them, and re-layouts  2.29 us (2%)
    pallas_call x1, Pallas kernels, per_device(): pl.pallas_call(kernel, out_shape=jax.ShapeDtypeStruct(queries.shape, BF16...  90.1 us
    unnamed x1, local copies, waits for them, and re-layouts  2.29 us

profile of v2, /device:TPU:25, one launch (start us, length us, event | category | flops | bytes accessed | tf_op | source)
XLA Modules:
  0.0 92.4 jit_solution(13158278736451103068)
XLA Ops:
  0.0 90.1 %causal_attention.1 = bf16[128,4096]{1,0:T(8,128)(2,1)} custom-call(bf16[128,4096]{1,0:T(8,128)(2,1)} %q_ref.1, bf16[128,1024]{1,0:T(8,128)(2,1)} %k_ref.1, bf16[128,1024]{1,0:T(8,128)(2,1)} %v_ref.1), custom_call_target="tpu_custom_call" | custom-call | tf_op jit(solution)/shard_map/causal_attention/pallas_call | solution.py:350
  90.1 2.3 %copy.5 = bf16[128,4096]{1,0:T(8,128)(2,1)} copy(bf16[128,4096]{1,0:T(8,128)(2,1)} %causal_attention.1) | data formatting | bytes 2097152

commit v3 on v2

v3 whole, which is shorter than its diff:
```python
import functools

import jax
import jax.numpy as jnp
from jax import lax
from jax.experimental import pallas as pl
from jax.experimental.pallas import tpu as pltpu
from jax.sharding import PartitionSpec as P

BLOCK = 128
WIDTH = 128
GROUP = 4 * WIDTH
ROWS = 4 * BLOCK
CHUNK = 1024
PART = 2048
SPAN = 256
SLOTS = 8
LOG2_SCALE = WIDTH**-0.5 * 1.4426950408889634
MESH = pl.DeviceIdType.MESH
F32 = jnp.float32
BF16 = jnp.bfloat16


def kernel(
    q_ref, k_ref, v_ref, out_ref,
    kv, kv_out, v_raw, q_in, q_pair, peak, total, acc, score_a, score_b, top_a, top_b, o_buf,
    local_sem, load_sem, home_send, home_recv, mate_send, mate_recv, core_send, core_recv, out_send, out_recv,
):
    y = lax.axis_index("ctx")
    head = lax.axis_index("head")
    x, z, c = head // 8, lax.rem(head, 8) // 2, lax.rem(head, 2)
    low_y, low_x, low_z = (lax.min(v, 3 - v) for v in (y, x, z))
    high_y, high_x, high_z = (v // 2 for v in (y, x, z))
    my_slot = my_head = 4 * high_y + 2 * high_x + high_z
    my_chunk, my_row = 4 * high_y + high_x, 4 * c + high_z

    def at(y_, x_, z_, c_):
        return (y_, x_ * 8 + z_ * 2 + c_)

    def beside(v):
        return v + 1 - 2 * lax.rem(v, 2)

    homes = []
    for flip in range(7, 0, -1):
        y_, x_, z_ = (3 - v if flip & bit else v for v, bit in ((y, 4), (x, 2), (z, 1)))
        homes.append((4 * (y_ // 2) + 2 * (x_ // 2) + z_ // 2, at(y_, x_, z_, c)))
    mate_y, mate_x, mate_z = at(beside(y), x, z, c), at(y, beside(x), z, c), at(y, x, beside(z), c)
    twin = at(y, x, z, 1 - c)

    barrier = pltpu.get_barrier_semaphore()
    for other in [to for _, to in homes] + [mate_y, mate_x, mate_z, twin]:
        pl.semaphore_signal(barrier, inc=1, device_id=other, device_id_type=MESH)

    def columns(head_, width):
        return pl.ds(pl.multiple_of(head_ * width, width), width)

    load_v = pltpu.make_async_copy(v_ref, v_raw, local_sem.at[0])
    load_v.start()
    load_k = [
        pltpu.make_async_copy(k_ref.at[:, h * WIDTH : (h + 1) * WIDTH], kv_out.at[h, 0], load_sem.at[h]) for h in range(8)
    ]
    for copy in load_k:
        copy.start()
    own = [pltpu.make_async_copy(q_ref.at[:, columns(my_head, GROUP)], q_in.at[my_slot], local_sem.at[1])]
    own[0].start()
    peak[...] = jnp.full_like(peak, -1e30)
    total[...] = jnp.zeros_like(total)
    acc[...] = jnp.zeros_like(acc)
    load_v.wait()
    for h in range(8):
        kv_out[h, 1] = v_raw[:, h * WIDTH : (h + 1) * WIDTH].T
    for copy in load_k:
        copy.wait()
    own.append(pltpu.make_async_copy(kv_out.at[my_head], kv.at[my_chunk, my_row], local_sem.at[2]))
    own[-1].start()

    pl.semaphore_wait(barrier, 11)

    home, mates, core = (home_send, home_recv), (mate_send, mate_recv), (core_send, core_recv)
    sent = {}

    def send(src, dst, sems, index, device, recv_index=None, noted=None):
        send_sem, recv_sem = sems
        pltpu.make_async_remote_copy(
            src_ref=src,
            dst_ref=dst,
            send_sem=send_sem.at[index],
            recv_sem=recv_sem.at[index if recv_index is None else recv_index],
            device_id=device,
            device_id_type=MESH,
        ).start()
        sent[id(send_sem), noted or index] = (send_sem, src.shape)

    def arrived(dst, recv_sem):
        pltpu.make_async_remote_copy(
            src_ref=dst, dst_ref=dst, send_sem=local_sem.at[0], recv_sem=recv_sem, device_id=twin, device_id_type=MESH
        ).wait_recv()

    def send_kv():
        for i, (there, to) in enumerate(homes):
            send(kv_out.at[there], kv.at[my_chunk, my_row], home, (0, i), to, (0, my_slot))

    pl.when(high_y == 0)(send_kv)
    for i, (there, to) in enumerate(homes):
        send(q_ref.at[:, columns(there, GROUP)], q_in.at[my_slot], home, (1, i), to, (1, my_slot))
    pl.when(high_y == 1)(send_kv)

    for copy in own:
        copy.wait()

    def piece(quarter, chunk, chunks, mz, rows, c_=c):
        return kv.at[pl.ds(4 * quarter + chunk, chunks), pl.ds(4 * c_ + 2 * mz, rows)]

    def block(quarter, chunk, row, c_=c):
        return kv.at[4 * quarter + chunk, 4 * c_ + row]

    def pass_on(src, dst, quarter, number, device):
        send(src, dst, mates, (quarter, number), device)

    def to_twin(quarter, number, *what):
        send(piece(quarter, *what), piece(quarter, *what), core, (quarter, number), twin)

    def got(quarter, number, *what):
        arrived(piece(quarter, *what), mate_recv.at[quarter, number])

    def of_twin(quarter, number, *what):
        arrived(piece(quarter, *what, 1 - c), core_recv.at[quarter, number])

    def own_1(q):
        for i, (dx, dz) in enumerate(((0, 0), (0, 1), (1, 0), (1, 1))):
            hx, hz = lax.rem(high_x + dx, 2), lax.rem(high_z + dz, 2)
            this, there, slot = block(q, hx, hz), 2 * hx + hz, 4 * q + 2 * hx + hz

            @pl.when(slot != my_slot)
            def _():
                arrived(this, home_recv.at[0, slot])

            send(this, block(q, hx, 2 + hz), mates, (q, 4 + there), mate_z, noted=(q, 4 + i))
            send(this, block(q, 2 + hx, hz), mates, (q, there), mate_x, noted=(q, i))
            send(this, this, core, (q, there), twin, noted=(q, i))
            send(this, block(2 + q, hx, hz), mates, (2 + q, there), mate_y, noted=(2 + q, i))

    def own_2(q):
        for i in range(4):
            arrived(block(q, i // 2, 2 + i % 2), mate_recv.at[q, 4 + i])
        to_twin(q, 4, 0, 2, 1, 2)
        pass_on(piece(q, 1, 1, 1, 2), piece(q, 3, 1, 1, 2), q, 8, mate_x)
        pass_on(piece(q, 1, 1, 1, 2), piece(2 + q, 1, 1, 1, 2), 2 + q, 4, mate_y)

    def own_3(q):
        for i in range(4):
            arrived(block(q, 2 + i // 2, i % 2), mate_recv.at[q, i])
        pass_on(piece(q, 2, 1, 0, 2), piece(q, 2, 1, 1, 2), q, 9, mate_z)
        to_twin(q, 5, 2, 2, 0, 2)
        pass_on(piece(q, 2, 1, 0, 2), piece(2 + q, 2, 1, 0, 2), 2 + q, 5, mate_y)

    def own_4(q):
        got(q, 8, 3, 1, 1, 2)
        got(q, 9, 2, 1, 1, 2)
        to_twin(q, 6, 2, 2, 1, 2)

    def own_twin_1(q):
        for i in range(4):
            arrived(block(q, i // 2, i % 2, 1 - c), core_recv.at[q, i])
        of_twin(q, 4, 0, 2, 1, 2)

    def own_twin_2(q):
        of_twin(q, 5, 2, 2, 0, 2)
        of_twin(q, 6, 2, 2, 1, 2)

    def mate_1(q):
        q = 2 + q
        for i in range(4):
            arrived(block(q, i // 2, i % 2), mate_recv.at[q, i])
        pass_on(piece(q, 0, 1, 0, 2), piece(q, 0, 1, 1, 2), q, 6, mate_z)
        pass_on(piece(q, 1, 1, 0, 2), piece(q, 3, 1, 0, 2), q, 7, mate_x)
        to_twin(q, 0, 0, 2, 0, 2)

    def mate_2(q):
        q = 2 + q
        got(q, 5, 2, 1, 0, 2)
        pass_on(piece(q, 2, 1, 0, 2), piece(q, 2, 1, 1, 2), q, 8, mate_z)
        to_twin(q, 1, 2, 1, 0, 2)
        got(q, 4, 1, 1, 1, 2)
        pass_on(piece(q, 1, 1, 1, 2), piece(q, 3, 1, 1, 2), q, 9, mate_x)
        to_twin(q, 2, 1, 1, 1, 2)

    def mate_3(q):
        q = 2 + q
        got(q, 6, 0, 1, 1, 2)
        to_twin(q, 3, 0, 1, 1, 2)

    def mate_4(q):
        q = 2 + q
        got(q, 7, 3, 1, 0, 2)
        to_twin(q, 4, 3, 1, 0, 2)
        got(q, 8, 2, 1, 1, 2)
        to_twin(q, 5, 2, 1, 1, 2)
        got(q, 9, 3, 1, 1, 2)
        to_twin(q, 6, 3, 1, 1, 2)

    def mate_twin_1(q):
        q = 2 + q
        of_twin(q, 0, 0, 2, 0, 2)
        of_twin(q, 2, 1, 1, 1, 2)
        of_twin(q, 3, 0, 1, 1, 2)

    def mate_twin_2(q):
        q = 2 + q
        for number, (chunk, mz) in ((1, (2, 0)), (4, (3, 0)), (5, (2, 1)), (6, (3, 1))):
            of_twin(q, number, chunk, 1, mz, 2)

    def split_queries(slot):
        @pl.when(slot != my_slot)
        def _():
            arrived(q_in.at[slot], home_recv.at[1, slot])

        for h in range(4):
            scaled = q_in[slot, :, h * WIDTH : (h + 1) * WIDTH].astype(F32) * LOG2_SCALE
            first = scaled.astype(BF16)
            q_pair[slot, h * BLOCK : (h + 1) * BLOCK, :WIDTH] = first
            q_pair[slot, h * BLOCK : (h + 1) * BLOCK, WIDTH:] = (scaled - first.astype(F32)).astype(BF16)

    order = []
    for z_ in range(4):
        mz = low_z if min(z_, 3 - z_) == 0 else 1 - low_z
        order += [4 * c_ + 2 * mz + z_ // 2 for c_ in range(2)]

    def parts(chunks):
        blocks = [(chunk, row) for chunk in chunks for row in order]
        return [blocks[i : i + PART // BLOCK] for i in range(0, len(blocks), PART // BLOCK)]

    def work(ahead, behind):
        ahead_parts = parts(ahead[1]) if ahead else []
        behind_parts = parts(behind[1]) if behind else []
        for start in range(0, ROWS, SPAN):
            columns_ = slice(start, start + SPAN)
            if behind:
                slot, _, src, src_top = behind
                old = peak[slot, :, columns_]
                new = jnp.maximum(old, jnp.max(src_top[:, columns_], axis=0, keepdims=True))
                rescale = jnp.exp2(old - new)
                peak[slot, :, columns_] = new
                sums, mixture = total[slot, :, columns_] * rescale, None
            highest = None
            for i in range(max(len(ahead_parts), len(behind_parts))):
                if i < len(ahead_parts):
                    slot_, chunks_, dst, dst_top, offset = ahead
                    k = jnp.concatenate([kv[chunk, b, 0] for chunk, b in ahead_parts[i]], axis=0)
                    rows = slice(i * PART, i * PART + k.shape[0])
                    s = lax.dot_general(
                        jnp.concatenate([k, k], axis=1), q_pair[slot_, columns_], (((1,), (1,)), ((), ())),
                        preferred_element_type=F32,
                    )
                    if offset is not None and rows.stop > CHUNK * (len(chunks_) - 1):
                        past = rows.start - CHUNK * (len(chunks_) - 1)
                        key = past + lax.broadcasted_iota(jnp.int32, s.shape, 0)
                        token = lax.rem(lax.broadcasted_iota(jnp.int32, s.shape, 1), BLOCK)
                        s = jnp.where(key <= token + offset, s, -1e30)
                    dst[rows, columns_] = s
                    best = jnp.max(s.reshape(-1, 8, SPAN), axis=0)
                    highest = best if highest is None else jnp.maximum(highest, best)
                if i < len(behind_parts):
                    rows = slice(i * PART, i * PART + BLOCK * len(behind_parts[i]))
                    weights = jnp.exp2(src[rows, columns_] - new)
                    sums = sums + jnp.sum(weights.reshape(-1, 8, SPAN), axis=0)
                    v = jnp.concatenate([kv[chunk, b, 1] for chunk, b in behind_parts[i]], axis=1)
                    term = jnp.dot(v, weights.astype(BF16), preferred_element_type=F32)
                    mixture = term if mixture is None else mixture + term
            if ahead:
                dst_top[:, columns_] = highest
            if behind:
                total[slot, :, columns_] = sums
                acc[slot, :, columns_] = acc[slot, :, columns_] * rescale + mixture

    def finish(slot):
        for h in range(4):
            columns_ = slice(h * BLOCK, (h + 1) * BLOCK)
            part = acc[slot, :, columns_] / jnp.sum(total[slot, :, columns_], axis=0, keepdims=True)
            o_buf[slot, :, h * WIDTH : (h + 1) * WIDTH] = part.T.astype(BF16)

        @pl.when(slot != my_slot)
        def _():
            pltpu.make_async_remote_copy(
                src_ref=o_buf.at[slot],
                dst_ref=out_ref.at[:, columns(my_head, GROUP)],
                send_sem=out_send.at[slot],
                recv_sem=out_recv.at[my_head],
                device_id=at(
                    low_y + slot // 4 * (3 - 2 * low_y),
                    low_x + lax.rem(slot, 4) // 2 * (3 - 2 * low_x),
                    low_z + lax.rem(slot, 2) * (3 - 2 * low_z),
                    c,
                ),
                device_id_type=MESH,
            ).start()

        @pl.when(slot == my_slot)
        def _():
            pltpu.make_async_copy(o_buf.at[slot], out_ref.at[:, columns(my_head, GROUP)], local_sem.at[0]).start()

    def lower_queries(_):
        for slot in range(4):
            split_queries(slot)

    own_1(0)
    own_2(0)
    own_3(0)
    for slot in range(4, 8):
        split_queries(slot)
    own_twin_1(0)

    def side_of(k):
        return lax.rem(high_z + 3 - k, 2)

    def lead_edge(r, k):
        return 4 * r + 2 + side_of(k), (4 * r, 4 * r + 2)

    def wide_edge(r, k):
        return 4 * r + 2 * (1 - low_x) + side_of(k), (4 * r + 3 - low_x, 4 * r + 1 - low_x)

    def narrow_edge(r, k):
        return 4 * r + 2 * low_x + side_of(k), (4 * r + low_x,)

    def offset_of(k):
        return BLOCK * (2 * (low_z + side_of(k) * (3 - 2 * low_z)) + c)

    def among(r, k, m):
        upper, quarter = 1 - (1 - r) * low_y, 2 + r * (1 - low_y)
        hx = low_x if m < 2 else 1 - low_x
        chunk = 4 * quarter + 2 * (m % 2)
        return 4 * upper + 2 * hx + side_of(k), (chunk, chunk + 1)

    def pick(first, one, other):
        (slot, (a_, b_)), (slot_, (c_, d_)) = one, other
        return jnp.where(first, slot, slot_), (jnp.where(first, a_, c_), jnp.where(first, b_, d_))

    def unit(r, j):
        past = j - (8 - 8 * r)
        first = 2 * (lax.rem(j, 8) // 4)
        later = pick(past < 2, lead_edge(r, past), among(r, 0, 0))
        return pick(past < 0, (4 + lax.rem(j, 4), (first, first + 1)), later)

    steps = {
        0: [(own_4, 0), (mate_1, 0)],
        1: [(own_twin_2, 0), (mate_2, 0)],
        2: [(own_1, 1)],
        3: [(mate_3, 0), (mate_4, 0), (lower_queries, 0)],
        4: [(mate_twin_1, 0), (own_2, 1), (own_3, 1)],
        5: [(mate_4, 1), (mate_twin_1, 1)],
    }
    places = {
        (0, 0, 0): [(mate_twin_2, 0), (mate_1, 1)],
        (0, 0, 1): [(mate_2, 1), (own_4, 1)],
        (0, 1, 1): [(own_twin_1, 1), (own_twin_2, 1), (mate_3, 1)],
        (1, 0, 0): [(mate_twin_2, 1)],
    }

    def do(actions):
        def run():
            for action, quarter in actions:
                action(quarter)

        return run

    a, b = (score_a, top_a), (score_b, top_b)
    zero = jnp.int32(0)
    work((*unit(zero, zero), *a, None), None)

    def full(r, i, _):
        for step, actions in steps.items():
            pl.when(i + 5 * r == step)(do(actions))
        work((*unit(r, 2 * i + 1), *b, None), (*unit(r, 2 * i), *a))
        work((*unit(r, 2 * i + 2), *a, None), (*unit(r, 2 * i + 1), *b))
        return 0

    def slots(r, k, _):
        def at_place(number):
            for (r_, k_, number_), actions in places.items():
                if number_ == number:
                    pl.when((r == r_) & (k == k_))(do(actions))

        offset = offset_of(k)
        wide, narrow = wide_edge(r, k), narrow_edge(r, k)
        after = pick(k == 0, among(r, 1, 0), lead_edge(1, 0))
        at_place(0)
        work((*among(r, k, 1), *b, None), (*among(r, k, 0), *a))
        work((*narrow, *a, offset), (*among(r, k, 1), *b))
        work((*among(r, k, 2), *b, None), (*narrow, *a))
        finish(narrow[0])
        at_place(1)
        work((*among(r, k, 3), *a, None), (*among(r, k, 2), *b))
        work((*wide, *b, offset), (*among(r, k, 3), *a))
        work((*after, *a, None), (*wide, *b))
        finish(wide[0])
        return 0

    def round_(r, _):
        lax.fori_loop(0, 5 - 4 * r, functools.partial(full, r), 0)
        lax.fori_loop(0, 2, functools.partial(slots, r), 0)
        return 0

    lax.fori_loop(0, 2, round_, 0)

    for (_, index), (send_sem, shape) in sent.items():
        held = {
            (BLOCK, GROUP): q_in.at[0],
            (2, BLOCK, WIDTH): kv.at[0, 0],
            (1, 2, 2, BLOCK, WIDTH): kv.at[pl.ds(0, 1), pl.ds(0, 2)],
            (2, 2, 2, BLOCK, WIDTH): kv.at[pl.ds(0, 2), pl.ds(0, 2)],
        }[shape]
        pltpu.make_async_remote_copy(
            src_ref=held, dst_ref=held, send_sem=send_sem.at[index], recv_sem=local_sem.at[0], device_id=twin,
            device_id_type=MESH,
        ).wait_send()
    for slot in range(SLOTS):

        @pl.when(slot != my_slot)
        def _():
            done = pltpu.make_async_remote_copy(
                src_ref=o_buf.at[slot],
                dst_ref=out_ref.at[:, pl.ds(slot * GROUP, GROUP)],
                send_sem=out_send.at[slot],
                recv_sem=out_recv.at[slot],
                device_id=twin,
                device_id_type=MESH,
            )
            done.wait_send()
            done.wait_recv()

        @pl.when(slot == my_slot)
        def _():
            pltpu.make_async_copy(o_buf.at[slot], out_ref.at[:, columns(my_head, GROUP)], local_sem.at[0]).wait()


def per_device(queries, keys, values):
    sem = pltpu.SemaphoreType.DMA
    return pl.pallas_call(
        kernel,
        out_shape=jax.ShapeDtypeStruct(queries.shape, BF16),
        in_specs=[pl.BlockSpec(memory_space=pl.ANY)] * 3,
        out_specs=pl.BlockSpec(memory_space=pl.ANY),
        scratch_shapes=[
            pltpu.VMEM((16, 8, 2, BLOCK, WIDTH), BF16),
            pltpu.VMEM((8, 2, BLOCK, WIDTH), BF16),
            pltpu.VMEM((BLOCK, 8 * WIDTH), BF16),
            pltpu.VMEM((SLOTS, BLOCK, GROUP), BF16),
            pltpu.VMEM((SLOTS, ROWS, 2 * WIDTH), BF16),
            pltpu.VMEM((SLOTS, 1, ROWS), F32),
            pltpu.VMEM((SLOTS, 8, ROWS), F32),
            pltpu.VMEM((SLOTS, WIDTH, ROWS), F32),
            pltpu.VMEM((2 * CHUNK, ROWS), F32),
            pltpu.VMEM((2 * CHUNK, ROWS), F32),
            pltpu.VMEM((8, ROWS), F32),
            pltpu.VMEM((8, ROWS), F32),
            pltpu.VMEM((SLOTS, BLOCK, GROUP), BF16),
            sem((4,)), sem((8,)),
            sem((2, 7)), sem((2, 8)),
            sem((4, 10)), sem((4, 10)),
            sem((4, 7)), sem((4, 7)),
            sem((8,)), sem((8,)),
        ],
        compiler_params=pltpu.CompilerParams(
            collective_id=0, has_side_effects=True, vmem_limit_bytes=56 * 2**20
        ),
        name="causal_attention",
    )(queries, keys, values)


def solution(mesh):
    spec = P(("ctx", "head"), None)
    return jax.shard_map(per_device, mesh=mesh, in_specs=(spec, spec, spec), out_specs=spec, check_vma=False)
```

time: 92.6 us -> 81.3 us (0.88)
  the two profiles are of different devices: /device:TPU:25 before, /device:TPU:22 now
where the time goes in v3:
time: 81.3 us; the launch traced here: 81.1 us
  Pallas kernels  78.8 us (97%)
  local copies, waits for them, and re-layouts  2.29 us (3%)
    pallas_call x1, Pallas kernels, per_device(): pl.pallas_call(kernel, out_shape=jax.ShapeDtypeStruct(queries.shape, BF16...  78.8 us
    unnamed x1, local copies, waits for them, and re-layouts  2.29 us

profile of v3, /device:TPU:22, one launch (start us, length us, event | category | flops | bytes accessed | tf_op | source)
XLA Modules:
  0.0 81.1 jit_solution(10012528757758619147)
XLA Ops:
  0.0 78.8 %causal_attention.1 = bf16[128,4096]{1,0:T(8,128)(2,1)} custom-call(bf16[128,4096]{1,0:T(8,128)(2,1)} %q_ref.1, bf16[128,1024]{1,0:T(8,128)(2,1)} %k_ref.1, bf16[128,1024]{1,0:T(8,128)(2,1)} %v_ref.1), custom_call_target="tpu_custom_call" | custom-call | tf_op jit(solution)/shard_map/causal_attention/pallas_call | solution.py:438
  78.8 2.3 %copy.5 = bf16[128,4096]{1,0:T(8,128)(2,1)} copy(bf16[128,4096]{1,0:T(8,128)(2,1)} %causal_attention.1) | data formatting | bytes 2097152

commit v4 on v3

--- a/solution.py
+++ b/solution.py
@@ -66,14 +66,6 @@
     peak[...] = jnp.full_like(peak, -1e30)
     total[...] = jnp.zeros_like(total)
     acc[...] = jnp.zeros_like(acc)
-    load_v.wait()
-    for h in range(8):
-        kv_out[h, 1] = v_raw[:, h * WIDTH : (h + 1) * WIDTH].T
-    for copy in load_k:
-        copy.wait()
-    own.append(pltpu.make_async_copy(kv_out.at[my_head], kv.at[my_chunk, my_row], local_sem.at[2]))
-    own[-1].start()
-
     pl.semaphore_wait(barrier, 11)
 
     home, mates, core = (home_send, home_recv), (mate_send, mate_recv), (core_send, core_recv)
@@ -96,15 +88,23 @@
             src_ref=dst, dst_ref=dst, send_sem=local_sem.at[0], recv_sem=recv_sem, device_id=twin, device_id_type=MESH
         ).wait_recv()
 
+    def send_queries():
+        for i, (there, to) in enumerate(homes):
+            send(q_ref.at[:, columns(there, GROUP)], q_in.at[my_slot], home, (1, i), to, (1, my_slot))
+
     def send_kv():
         for i, (there, to) in enumerate(homes):
             send(kv_out.at[there], kv.at[my_chunk, my_row], home, (0, i), to, (0, my_slot))
 
+    pl.when(high_y == 1)(send_queries)
+    load_v.wait()
+    for h in range(8):
+        kv_out[h, 1] = v_raw[:, h * WIDTH : (h + 1) * WIDTH].T
+    for copy in load_k:
+        copy.wait()
     pl.when(high_y == 0)(send_kv)
-    for i, (there, to) in enumerate(homes):
-        send(q_ref.at[:, columns(there, GROUP)], q_in.at[my_slot], home, (1, i), to, (1, my_slot))
-    pl.when(high_y == 1)(send_kv)
-
+    own.append(pltpu.make_async_copy(kv_out.at[my_head], kv.at[my_chunk, my_row], local_sem.at[2]))
+    own[-1].start()
     for copy in own:
         copy.wait()
 
@@ -304,8 +304,10 @@
             split_queries(slot)
 
     own_1(0)
+    pl.when(high_y == 0)(send_queries)
     own_2(0)
     own_3(0)
+    pl.when(high_y == 1)(send_kv)
     for slot in range(4, 8):
         split_queries(slot)
     own_twin_1(0)
@@ -325,9 +327,11 @@
     def offset_of(k):
         return BLOCK * (2 * (low_z + side_of(k) * (3 - 2 * low_z)) + c)
 
+    narrow_last = lax.rem(high_x + low_x + 1, 2)
+
     def among(r, k, m):
         upper, quarter = 1 - (1 - r) * low_y, 2 + r * (1 - low_y)
-        hx = low_x if m < 2 else 1 - low_x
+        hx = 1 - high_x if m < 2 else high_x
         chunk = 4 * quarter + 2 * (m % 2)
         return 4 * upper + 2 * hx + side_of(k), (chunk, chunk + 1)
 
@@ -342,16 +346,17 @@
         return pick(past < 0, (4 + lax.rem(j, 4), (first, first + 1)), later)
 
     steps = {
-        0: [(own_4, 0), (mate_1, 0)],
-        1: [(own_twin_2, 0), (mate_2, 0)],
+        0: [(mate_1, 0)],
+        1: [(own_4, 0), (mate_2, 0)],
         2: [(own_1, 1)],
         3: [(mate_3, 0), (mate_4, 0), (lower_queries, 0)],
-        4: [(mate_twin_1, 0), (own_2, 1), (own_3, 1)],
+        4: [(mate_twin_1, 0)],
         5: [(mate_4, 1), (mate_twin_1, 1)],
     }
     places = {
-        (0, 0, 0): [(mate_twin_2, 0), (mate_1, 1)],
-        (0, 0, 1): [(mate_2, 1), (own_4, 1)],
+        (0, 0, 0): [(mate_twin_2, 0), (own_2, 1), (own_3, 1)],
+        (0, 0, 1): [(mate_1, 1), (own_4, 1)],
+        (0, 1, 0): [(mate_2, 1)],
         (0, 1, 1): [(own_twin_1, 1), (own_twin_2, 1), (mate_3, 1)],
         (1, 0, 0): [(mate_twin_2, 1)],
     }
@@ -371,6 +376,7 @@
         for step, actions in steps.items():
             pl.when(i + 5 * r == step)(do(actions))
         work((*unit(r, 2 * i + 1), *b, None), (*unit(r, 2 * i), *a))
+        pl.when(i + 5 * r == 1)(do([(own_twin_2, 0)]))
         work((*unit(r, 2 * i + 2), *a, None), (*unit(r, 2 * i + 1), *b))
         return 0
 
@@ -381,18 +387,23 @@
                     pl.when((r == r_) & (k == k_))(do(actions))
 
         offset = offset_of(k)
-        wide, narrow = wide_edge(r, k), narrow_edge(r, k)
+        edges = narrow_edge(r, k), wide_edge(r, k)
         after = pick(k == 0, among(r, 1, 0), lead_edge(1, 0))
-        at_place(0)
-        work((*among(r, k, 1), *b, None), (*among(r, k, 0), *a))
-        work((*narrow, *a, offset), (*among(r, k, 1), *b))
-        work((*among(r, k, 2), *b, None), (*narrow, *a))
-        finish(narrow[0])
-        at_place(1)
-        work((*among(r, k, 3), *a, None), (*among(r, k, 2), *b))
-        work((*wide, *b, offset), (*among(r, k, 3), *a))
-        work((*after, *a, None), (*wide, *b))
-        finish(wide[0])
+
+        def visit(one, two):
+            at_place(0)
+            work((*among(r, k, 1), *b, None), (*among(r, k, 0), *a))
+            work((*one, *a, offset), (*among(r, k, 1), *b))
+            work((*among(r, k, 2), *b, None), (*one, *a))
+            finish(one[0])
+            at_place(1)
+            work((*among(r, k, 3), *a, None), (*among(r, k, 2), *b))
+            work((*two, *b, offset), (*among(r, k, 3), *a))
+            work((*after, *a, None), (*two, *b))
+            finish(two[0])
+
+        pl.when(narrow_last == 0)(lambda: visit(*edges))
+        pl.when(narrow_last == 1)(lambda: visit(*edges[::-1]))
         return 0
 
     def round_(r, _):
@@ -437,9 +448,9 @@
     sem = pltpu.SemaphoreType.DMA
     return pl.pallas_call(
         kernel,
-        out_shape=jax.ShapeDtypeStruct(queries.shape, BF16),
+        out_shape=pltpu.VMEM(queries.shape, BF16),
         in_specs=[pl.BlockSpec(memory_space=pl.ANY)] * 3,
-        out_specs=pl.BlockSpec(memory_space=pl.ANY),
+        out_specs=pl.BlockSpec(memory_space=pltpu.VMEM),
         scratch_shapes=[
             pltpu.VMEM((16, 8, 2, BLOCK, WIDTH), BF16),
             pltpu.VMEM((8, 2, BLOCK, WIDTH), BF16),

time: 81.3 us -> 74.4 us (0.915)
  the two profiles are of different devices: /device:TPU:22 before, /device:TPU:25 now
where the time goes in v4:
time: 74.4 us; the launch traced here: 74.2 us
  Pallas kernels  73.2 us (98%)
  local copies, waits for them, and re-layouts  0.97 us (1%)
    pallas_call x1, Pallas kernels, per_device(): pl.pallas_call(kernel, out_shape=pltpu.VMEM(queries.shape, BF16), in_spec...  73.2 us

profile of v4, /device:TPU:25, one launch (start us, length us, event | category | flops | bytes accessed | tf_op | source)
XLA Modules:
  0.0 74.2 jit_solution(16172343738077764389)
XLA Ops:
  0.0 73.2 %causal_attention.1 = bf16[128,4096]{1,0:T(8,128)(2,1)S(1)} custom-call(bf16[128,4096]{1,0:T(8,128)(2,1)} %q_ref.1, bf16[128,1024]{1,0:T(8,128)(2,1)} %k_ref.1, bf16[128,1024]{1,0:T(8,128)(2,1)} %v_ref.1), custom_call_target="tpu_custom_call" | custom-call | tf_op jit(solution)/shard_map/causal_attention/pallas_call | solution.py:449
  73.2 1.0 %copy.5 = bf16[128,4096]{1,0:T(8,128)(2,1)} copy(bf16[128,4096]{1,0:T(8,128)(2,1)S(1)} %causal_attention.1) | data formatting | bytes 2097152

commit v5 on v4

v5 whole, which is shorter than its diff:
```python
import functools

import jax
import jax.numpy as jnp
from jax import lax
from jax.experimental import pallas as pl
from jax.experimental.pallas import tpu as pltpu
from jax.sharding import PartitionSpec as P

BLOCK = 128
WIDTH = 128
GROUP = 4 * WIDTH
ROWS = 4 * BLOCK
CHUNK = 1024
AHEAD = 2048
BEHIND = 512
SPAN = 256
SLOTS = 8
LOG2_SCALE = WIDTH**-0.5 * 1.4426950408889634
MESH = pl.DeviceIdType.MESH
F32 = jnp.float32
BF16 = jnp.bfloat16


def kernel(
    q_ref, k_ref, v_ref, out_ref,
    kv, kv_out, v_raw, q_in, q_pair, peak, total, acc, score_a, score_b, top_a, top_b, o_buf,
    local_sem, load_sem, own_sem, home_send, home_recv, mate_send, mate_recv, core_send, core_recv, out_send, out_recv,
):
    y = lax.axis_index("ctx")
    head = lax.axis_index("head")
    x, z, c = head // 8, lax.rem(head, 8) // 2, lax.rem(head, 2)
    low_y, low_x, low_z = (lax.min(v, 3 - v) for v in (y, x, z))
    high_y, high_x, high_z = (v // 2 for v in (y, x, z))
    my_slot = my_head = 4 * high_y + 2 * high_x + high_z
    my_chunk, my_row = 4 * high_y + high_x, 4 * c + high_z

    def at(y_, x_, z_, c_):
        return (y_, x_ * 8 + z_ * 2 + c_)

    def beside(v):
        return v + 1 - 2 * lax.rem(v, 2)

    homes = []
    for flip in range(7, 0, -1):
        y_, x_, z_ = (3 - v if flip & bit else v for v, bit in ((y, 4), (x, 2), (z, 1)))
        homes.append((4 * (y_ // 2) + 2 * (x_ // 2) + z_ // 2, at(y_, x_, z_, c)))
    mate_y, mate_x, mate_z = at(beside(y), x, z, c), at(y, beside(x), z, c), at(y, x, beside(z), c)
    twin = at(y, x, z, 1 - c)

    barrier = pltpu.get_barrier_semaphore()
    for other in [to for _, to in homes] + [mate_y, mate_x, mate_z, twin]:
        pl.semaphore_signal(barrier, inc=1, device_id=other, device_id_type=MESH)

    def columns(head_, width):
        return pl.ds(pl.multiple_of(head_ * width, width), width)

    load_v = pltpu.make_async_copy(v_ref, v_raw, local_sem.at[0])
    load_v.start()
    load_k = [
        pltpu.make_async_copy(k_ref.at[:, h * WIDTH : (h + 1) * WIDTH], kv_out.at[h, 0], load_sem.at[h]) for h in range(8)
    ]
    for copy in load_k:
        copy.start()
    own = [pltpu.make_async_copy(q_ref.at[:, columns(my_head, GROUP)], q_in.at[my_slot], local_sem.at[1])]
    own[0].start()
    peak[...] = jnp.full_like(peak, -1e30)
    total[...] = jnp.zeros_like(total)
    acc[...] = jnp.zeros_like(acc)
    pl.semaphore_wait(barrier, 11)

    home, mates, core = (home_send, home_recv), (mate_send, mate_recv), (core_send, core_recv)
    sent = {}

    def send(src, dst, sems, index, device, recv_index=None):
        send_sem, recv_sem = sems
        pltpu.make_async_remote_copy(
            src_ref=src,
            dst_ref=dst,
            send_sem=send_sem.at[index],
            recv_sem=recv_sem.at[index if recv_index is None else recv_index],
            device_id=device,
            device_id_type=MESH,
        ).start()
        sent[id(send_sem), index] = (send_sem, src.shape)

    def arrived(dst, recv_sem):
        pltpu.make_async_remote_copy(
            src_ref=dst, dst_ref=dst, send_sem=local_sem.at[0], recv_sem=recv_sem, device_id=twin, device_id_type=MESH
        ).wait_recv()

    def send_queries():
        for i, (there, to) in enumerate(homes):
            send(q_ref.at[:, columns(there, GROUP)], q_in.at[my_slot], home, (1, i), to, (1, my_slot))

    def send_kv():
        for i, (there, to) in enumerate(homes):
            send(kv_out.at[there], kv.at[my_chunk, my_row], home, (0, i), to, (0, my_slot))

    pl.when(high_y == 1)(send_queries)
    load_v.wait()
    for h in range(8):
        kv_out[h, 1] = v_raw[:, h * WIDTH : (h + 1) * WIDTH].T
    for copy in load_k:
        copy.wait()
    pl.when(high_y == 0)(send_kv)
    own.append(pltpu.make_async_copy(kv_out.at[my_head], kv.at[my_chunk, my_row], local_sem.at[2]))
    own[-1].start()
    for copy in own:
        copy.wait()

    def piece(quarter, chunk, chunks, mz, c_=c):
        return kv.at[pl.ds(4 * quarter + chunk, chunks), pl.ds(4 * c_ + 2 * mz, 2)]

    def pass_on(what, to_what, number, device):
        send(piece(*what), piece(*to_what), mates, (to_what[0], number), device)

    def to_twin(number, *what):
        send(piece(*what), piece(*what), core, (what[0], number), twin)

    def got(number, *what):
        arrived(piece(*what), mate_recv.at[what[0], number])

    def of_twin(number, *what):
        arrived(piece(*what, 1 - c), core_recv.at[what[0], number])

    def own_1(q):
        for hx in range(2):
            for hz in range(2):
                slot = 4 * q + 2 * hx + hz

                @pl.when(slot != my_slot)
                def _():
                    arrived(kv.at[4 * q + hx, 4 * c + hz], home_recv.at[0, slot])

            if hx == 0:
                pass_on((q, 0, 1, 0), (q, 2, 1, 0), 0, mate_x)
            else:
                pass_on((q, 1, 1, 0), (q, 1, 1, 1), 1, mate_z)
        to_twin(0, q, 0, 2, 0)
        pass_on((q, 1, 1, 0), (q, 3, 1, 0), 2, mate_x)
        pass_on((q, 0, 1, 0), (q, 0, 1, 1), 3, mate_z)
        pass_on((q, 0, 2, 0), (2 + q, 0, 2, 0), 0, mate_y)

    def own_2(q):
        got(0, q, 2, 1, 0)
        to_twin(1, q, 2, 1, 0)
        got(1, q, 1, 1, 1)
        to_twin(2, q, 1, 1, 1)
        pass_on((q, 2, 1, 0), (q, 2, 1, 1), 4, mate_z)
        pass_on((q, 1, 1, 1), (q, 3, 1, 1), 5, mate_x)
        pass_on((q, 2, 1, 0), (2 + q, 2, 1, 0), 1, mate_y)
        pass_on((q, 1, 1, 1), (2 + q, 1, 1, 1), 2, mate_y)

    def own_3(q):
        got(3, q, 0, 1, 1)
        to_twin(3, q, 0, 1, 1)
        got(2, q, 3, 1, 0)
        to_twin(4, q, 3, 1, 0)

    def own_4(q):
        got(4, q, 2, 1, 1)
        to_twin(5, q, 2, 1, 1)
        got(5, q, 3, 1, 1)
        to_twin(6, q, 3, 1, 1)

    def own_twin_1(q):
        of_twin(0, q, 0, 2, 0)
        of_twin(1, q, 2, 1, 0)
        of_twin(2, q, 1, 1, 1)

    def own_twin_2(q):
        for number, (chunk, mz) in enumerate(((0, 1), (3, 0), (2, 1), (3, 1))):
            of_twin(3 + number, q, chunk, 1, mz)

    def mate_1(q):
        q = 2 + q
        got(0, q, 0, 2, 0)
        pass_on((q, 0, 1, 0), (q, 0, 1, 1), 3, mate_z)
        pass_on((q, 1, 1, 0), (q, 3, 1, 0), 4, mate_x)
        to_twin(0, q, 0, 2, 0)

    def mate_2(q):
        q = 2 + q
        got(1, q, 2, 1, 0)
        pass_on((q, 2, 1, 0), (q, 2, 1, 1), 5, mate_z)
        to_twin(1, q, 2, 1, 0)
        got(2, q, 1, 1, 1)
        pass_on((q, 1, 1, 1), (q, 3, 1, 1), 6, mate_x)
        to_twin(2, q, 1, 1, 1)

    def mate_3(q):
        q = 2 + q
        for number, (chunk, mz) in enumerate(((0, 1), (3, 0), (2, 1), (3, 1))):
            got(3 + number, q, chunk, 1, mz)
            to_twin(3 + number, q, chunk, 1, mz)

    def mate_twin_1(q):
        own_twin_1(2 + q)

    def mate_twin_2(q):
        own_twin_2(2 + q)

    def split_queries(slot):
        @pl.when(slot != my_slot)
        def _():
            arrived(q_in.at[slot], home_recv.at[1, slot])

        for h in range(4):
            scaled = q_in[slot, :, h * WIDTH : (h + 1) * WIDTH].astype(F32) * LOG2_SCALE
            first = scaled.astype(BF16)
            q_pair[slot, h * BLOCK : (h + 1) * BLOCK, :WIDTH] = first
            q_pair[slot, h * BLOCK : (h + 1) * BLOCK, WIDTH:] = (scaled - first.astype(F32)).astype(BF16)

    order = []
    for z_ in range(4):
        mz = low_z if min(z_, 3 - z_) == 0 else 1 - low_z
        order += [4 * c_ + 2 * mz + z_ // 2 for c_ in range(2)]

    def in_order(*chunks):
        return [(chunk, row) for chunk in chunks for row in order]

    def parts(blocks, size):
        return [blocks[i : i + size // BLOCK] for i in range(0, len(blocks), size // BLOCK)]

    def from_pairs(pairs):
        return [(chunk, 4 * c_ + 2 * mz + hz) for chunk, mz in pairs for c_ in range(2) for hz in range(2)]

    def work(ahead, behind, after_span=None):
        ahead_parts = parts(ahead[1], AHEAD) if ahead else []
        behind_parts = parts(behind[1], BEHIND) if behind else []
        for start in range(0, ROWS, SPAN):
            columns_ = slice(start, start + SPAN)
            if behind:
                slot, _, src, src_top = behind
                old = peak[slot, :, columns_]
                new = jnp.maximum(old, jnp.max(src_top[:, columns_], axis=0, keepdims=True))
                rescale = jnp.exp2(old - new)
                peak[slot, :, columns_] = new
                sums, mixture = total[slot, :, columns_] * rescale, None
            highest = None
            for i in range(max(len(ahead_parts), len(behind_parts))):
                if i < len(ahead_parts):
                    slot_, blocks_, dst, dst_top, offset = ahead
                    k = jnp.concatenate([kv[chunk, b, 0] for chunk, b in ahead_parts[i]], axis=0)
                    rows = slice(i * AHEAD, i * AHEAD + k.shape[0])
                    s = lax.dot_general(
                        jnp.concatenate([k, k], axis=1), q_pair[slot_, columns_], (((1,), (1,)), ((), ())),
                        preferred_element_type=F32,
                    )
                    if offset is not None and rows.stop > BLOCK * len(blocks_) - CHUNK:
                        past = rows.start + CHUNK - BLOCK * len(blocks_)
                        key = past + lax.broadcasted_iota(jnp.int32, s.shape, 0)
                        token = lax.rem(lax.broadcasted_iota(jnp.int32, s.shape, 1), BLOCK)
                        s = jnp.where(key <= token + offset, s, -1e30)
                    dst[rows, columns_] = s
                    best = jnp.max(s.reshape(-1, 8, SPAN), axis=0)
                    highest = best if highest is None else jnp.maximum(highest, best)
                if i < len(behind_parts):
                    rows = slice(i * BEHIND, i * BEHIND + BLOCK * len(behind_parts[i]))
                    weights = jnp.exp2(src[rows, columns_] - new)
                    sums = sums + jnp.sum(weights.reshape(-1, 8, SPAN), axis=0)
                    v = jnp.concatenate([kv[chunk, b, 1] for chunk, b in behind_parts[i]], axis=1)
                    term = jnp.dot(v, weights.astype(BF16), preferred_element_type=F32)
                    mixture = term if mixture is None else mixture + term
            if ahead:
                dst_top[:, columns_] = highest
            if behind:
                total[slot, :, columns_] = sums
                acc[slot, :, columns_] = acc[slot, :, columns_] * rescale + mixture
                if after_span is not None:
                    after_span(slot, start // SPAN)

    def result(slot, span):
        here = (slice(None), slice(span * SPAN, (span + 1) * SPAN))
        there = (slice(None), pl.ds(pl.multiple_of(my_head * GROUP + span * SPAN, SPAN), SPAN))
        return o_buf.at[(slot, *here)], out_ref.at[there]

    def finish_span(slot, span):
        for h in range(span * SPAN // BLOCK, (span + 1) * SPAN // BLOCK):
            columns_ = slice(h * BLOCK, (h + 1) * BLOCK)
            part = acc[slot, :, columns_] * (1.0 / jnp.sum(total[slot, :, columns_], axis=0, keepdims=True))
            o_buf[slot, :, h * WIDTH : (h + 1) * WIDTH] = part.T.astype(BF16)
        src, dst = result(slot, span)

        @pl.when(slot != my_slot)
        def _():
            pltpu.make_async_remote_copy(
                src_ref=src,
                dst_ref=dst,
                send_sem=out_send.at[slot, span],
                recv_sem=out_recv.at[my_head, span],
                device_id=at(
                    low_y + slot // 4 * (3 - 2 * low_y),
                    low_x + lax.rem(slot, 4) // 2 * (3 - 2 * low_x),
                    low_z + lax.rem(slot, 2) * (3 - 2 * low_z),
                    c,
                ),
                device_id_type=MESH,
            ).start()

        @pl.when(slot == my_slot)
        def _():
            pltpu.make_async_copy(src, dst, own_sem.at[span]).start()

    def finish(slot):
        for span in range(ROWS // SPAN):
            finish_span(slot, span)

    def lower_queries(_):
        for slot in range(4):
            split_queries(slot)

    own_1(0)
    pl.when(high_y == 0)(send_queries)
    own_2(0)
    pl.when(high_y == 1)(send_kv)
    split_queries(4)
    split_queries(5)
    own_twin_1(0)

    def side_of(k):
        return lax.rem(high_z + 3 - k, 2)

    def lead_edge(r, k):
        return 4 * r + 2 + side_of(k), [(4 * r, 0), (4 * r, 1), (4 * r + 2, 0), (4 * r + 2, 1)]

    def wide_edge(r, k):
        return 4 * r + 2 * (1 - low_x) + side_of(k), in_order(4 * r + 3 - low_x, 4 * r + 1 - low_x)

    def narrow_edge(r, k):
        return 4 * r + 2 * low_x + side_of(k), in_order(4 * r + low_x)

    def offset_of(k):
        return BLOCK * (2 * (low_z + side_of(k) * (3 - 2 * low_z)) + c)

    narrow_last = lax.rem(high_x + low_x + 1, 2)

    def half_of(quarter, part):
        return [
            (4 * quarter, part),
            (4 * quarter + 1 + part, part),
            (4 * quarter + 1 + 2 * part, 1 - part),
            (4 * quarter + 2 + part, part),
        ]

    def among(r, k, m):
        upper, quarter = 1 - (1 - r) * low_y, 2 + r * (1 - low_y)
        hx = 1 - high_x if m < 2 else high_x
        return 4 * upper + 2 * hx + side_of(k), half_of(quarter, m % 2)

    def pick(first, one, other):
        (slot, pairs), (slot_, pairs_) = one, other
        return jnp.where(first, slot, slot_), [
            tuple(jnp.where(first, v, w) for v, w in zip(p, p_, strict=True)) for p, p_ in zip(pairs, pairs_, strict=True)
        ]

    def unit(r, j):
        past = j - (8 - 8 * r)
        later = pick(past < 2, lead_edge(r, past), among(r, 0, 0))
        return pick(past < 0, (4 + lax.rem(j, 4), half_of(0, lax.rem(j, 8) // 4)), later)

    def whole(one):
        return one[0], from_pairs(one[1])

    steps = {
        1: [(split_queries, 7), (mate_1, 0), (own_4, 0)],
        2: [(mate_2, 0)],
        3: [(lower_queries, 0), (own_1, 1)],
        4: [(mate_3, 0), (mate_twin_1, 0)],
        5: [(mate_twin_1, 1)],
    }
    halfway = {0: [(split_queries, 6), (own_3, 0)], 1: [(own_twin_2, 0)], 5: [(mate_3, 1)]}
    places = {
        (0, 0, 0): [(mate_twin_2, 0)],
        (0, 0, 3): [(own_2, 1)],
        (0, 1, 0): [(own_3, 1), (mate_1, 1)],
        (0, 1, 1): [(own_4, 1), (mate_2, 1)],
        (0, 1, 2): [(own_twin_1, 1), (own_twin_2, 1)],
        (1, 0, 0): [(mate_twin_2, 1)],
    }

    def do(actions):
        def run():
            for action, quarter in actions:
                action(quarter)

        return run

    a, b = (score_a, top_a), (score_b, top_b)
    zero = jnp.int32(0)
    work((*whole(unit(zero, zero)), *a, None), None)

    def full(r, i, _):
        for step, actions in steps.items():
            pl.when(i + 5 * r == step)(do(actions))
        work((*whole(unit(r, 2 * i + 1)), *b, None), (*whole(unit(r, 2 * i)), *a))
        for step, actions in halfway.items():
            pl.when(i + 5 * r == step)(do(actions))
        work((*whole(unit(r, 2 * i + 2)), *a, None), (*whole(unit(r, 2 * i + 1)), *b))
        return 0

    def slots(r, k, _):
        def at_place(number):
            for (r_, k_, number_), actions in places.items():
                if number_ == number:
                    pl.when((r == r_) & (k == k_))(do(actions))

        offset = offset_of(k)
        edges = narrow_edge(r, k), wide_edge(r, k)
        after = whole(pick(k == 0, among(r, 1, 0), lead_edge(1, 0)))
        fills = [whole(among(r, k, m)) for m in range(4)]

        def visit(one, two):
            at_place(0)
            work((*fills[1], *b, None), (*fills[0], *a))
            at_place(3)
            work((*one, *a, offset), (*fills[1], *b))
            work((*fills[2], *b, None), (*one, *a))
            finish(one[0])
            at_place(1)
            work((*fills[3], *a, None), (*fills[2], *b))
            work((*two, *b, offset), (*fills[3], *a))
            at_place(2)
            pl.when(r + k < 2)(lambda: work((*after, *a, None), (*two, *b)))
            pl.when(r + k < 2)(lambda: finish(two[0]))
            pl.when(r + k == 2)(lambda: work(None, (*two, *b), finish_span))

        pl.when(narrow_last == 0)(lambda: visit(*edges))
        pl.when(narrow_last == 1)(lambda: visit(*edges[::-1]))
        return 0

    def round_(r, _):
        lax.fori_loop(0, 5 - 4 * r, functools.partial(full, r), 0)
        lax.fori_loop(0, 2, functools.partial(slots, r), 0)
        return 0

    lax.fori_loop(0, 2, round_, 0)

    for (_, index), (send_sem, shape) in sent.items():
        held = {
            (BLOCK, GROUP): q_in.at[0],
            (2, BLOCK, WIDTH): kv.at[0, 0],
            (1, 2, 2, BLOCK, WIDTH): kv.at[pl.ds(0, 1), pl.ds(0, 2)],
            (2, 2, 2, BLOCK, WIDTH): kv.at[pl.ds(0, 2), pl.ds(0, 2)],
        }[shape]
        pltpu.make_async_remote_copy(
            src_ref=held, dst_ref=held, send_sem=send_sem.at[index], recv_sem=local_sem.at[0], device_id=twin,
            device_id_type=MESH,
        ).wait_send()
    for slot in range(SLOTS):
        for span in range(ROWS // SPAN):
            src, dst = result(slot, span)

            @pl.when(slot != my_slot)
            def _():
                done = pltpu.make_async_remote_copy(
                    src_ref=src,
                    dst_ref=out_ref.at[:, pl.ds(slot * GROUP + span * SPAN, SPAN)],
                    send_sem=out_send.at[slot, span],
                    recv_sem=out_recv.at[slot, span],
                    device_id=twin,
                    device_id_type=MESH,
                )
                done.wait_send()
                done.wait_recv()

            @pl.when(slot == my_slot)
            def _():
                pltpu.make_async_copy(src, dst, own_sem.at[span]).wait()


def per_device(queries, keys, values):
    sem = pltpu.SemaphoreType.DMA
    return pl.pallas_call(
        kernel,
        out_shape=pltpu.VMEM(queries.shape, BF16),
        in_specs=[pl.BlockSpec(memory_space=pl.ANY)] * 3,
        out_specs=pl.BlockSpec(memory_space=pltpu.VMEM),
        scratch_shapes=[
            pltpu.VMEM((16, 8, 2, BLOCK, WIDTH), BF16),
            pltpu.VMEM((8, 2, BLOCK, WIDTH), BF16),
            pltpu.VMEM((BLOCK, 8 * WIDTH), BF16),
            pltpu.VMEM((SLOTS, BLOCK, GROUP), BF16),
            pltpu.VMEM((SLOTS, ROWS, 2 * WIDTH), BF16),
            pltpu.VMEM((SLOTS, 1, ROWS), F32),
            pltpu.VMEM((SLOTS, 8, ROWS), F32),
            pltpu.VMEM((SLOTS, WIDTH, ROWS), F32),
            pltpu.VMEM((2 * CHUNK, ROWS), F32),
            pltpu.VMEM((2 * CHUNK, ROWS), F32),
            pltpu.VMEM((8, ROWS), F32),
            pltpu.VMEM((8, ROWS), F32),
            pltpu.VMEM((SLOTS, BLOCK, GROUP), BF16),
            sem((4,)), sem((8,)), sem((2,)),
            sem((2, 7)), sem((2, 8)),
            sem((4, 7)), sem((4, 7)),
            sem((4, 7)), sem((4, 7)),
            sem((8, 2)), sem((8, 2)),
        ],
        compiler_params=pltpu.CompilerParams(
            collective_id=0, has_side_effects=True, vmem_limit_bytes=56 * 2**20
        ),
        name="causal_attention",
    )(queries, keys, values)


def solution(mesh):
    spec = P(("ctx", "head"), None)
    return jax.shard_map(per_device, mesh=mesh, in_specs=(spec, spec, spec), out_specs=spec, check_vma=False)
```

time: 74.4 us -> 73 us (0.981)
  Pallas kernels: 73.2 us -> 71.2 us
    pallas_call x1, Pallas kernels: 73.2 us -> 71.2 us  [per_device(): pl.pallas_call(kernel, out_shape=pltpu.VMEM(queries.shape, BF16), in_spec...]
where the time goes in v5:
time: 73 us; the launch traced here: 72.2 us
  Pallas kernels  71.2 us (98%)
  local copies, waits for them, and re-layouts  0.97 us (1%)
    pallas_call x1, Pallas kernels, per_device(): pl.pallas_call(kernel, out_shape=pltpu.VMEM(queries.shape, BF16), in_spec...  71.2 us

profile of v5, /device:TPU:25, one launch (start us, length us, event | category | flops | bytes accessed | tf_op | source)
XLA Modules:
  0.0 72.2 jit_solution(18395247794160958600)
XLA Ops:
  0.0 71.2 %causal_attention.1 = bf16[128,4096]{1,0:T(8,128)(2,1)S(1)} custom-call(bf16[128,4096]{1,0:T(8,128)(2,1)} %q_ref.1, bf16[128,1024]{1,0:T(8,128)(2,1)} %k_ref.1, bf16[128,1024]{1,0:T(8,128)(2,1)} %v_ref.1), custom_call_target="tpu_custom_call" | custom-call | tf_op jit(solution)/shard_map/causal_attention/pallas_call | solution.py:475
  71.2 1.0 %copy.5 = bf16[128,4096]{1,0:T(8,128)(2,1)} copy(bf16[128,4096]{1,0:T(8,128)(2,1)S(1)} %causal_attention.1) | data formatting | bytes 2097152

commit v6 on v5

--- a/solution.py
+++ b/solution.py
@@ -365,18 +365,21 @@
 
     steps = {
         1: [(split_queries, 7), (mate_1, 0), (own_4, 0)],
-        2: [(mate_2, 0)],
-        3: [(lower_queries, 0), (own_1, 1)],
+        2: [(mate_2, 0), (own_1, 1)],
         4: [(mate_3, 0), (mate_twin_1, 0)],
         5: [(mate_twin_1, 1)],
     }
-    halfway = {0: [(split_queries, 6), (own_3, 0)], 1: [(own_twin_2, 0)], 5: [(mate_3, 1)]}
+    halfway = {
+        0: [(split_queries, 6), (own_3, 0)],
+        1: [(own_twin_2, 0)],
+        3: [(lower_queries, 0)],
+    }
     places = {
-        (0, 0, 0): [(mate_twin_2, 0)],
-        (0, 0, 3): [(own_2, 1)],
-        (0, 1, 0): [(own_3, 1), (mate_1, 1)],
-        (0, 1, 1): [(own_4, 1), (mate_2, 1)],
-        (0, 1, 2): [(own_twin_1, 1), (own_twin_2, 1)],
+        (0, 0, 0): [(mate_twin_2, 0), (own_2, 1)],
+        (0, 0, 1): [(own_3, 1), (mate_1, 1)],
+        (0, 1, 0): [(own_4, 1)],
+        (0, 1, 3): [(mate_2, 1)],
+        (0, 1, 2): [(own_twin_1, 1), (own_twin_2, 1), (mate_3, 1)],
         (1, 0, 0): [(mate_twin_2, 1)],
     }
 

time: 73 us -> 71.9 us (0.985)
  no operation moved by 1% of the time
where the time goes in v6:
time: 71.9 us; the launch traced here: 71.6 us
  Pallas kernels  70.6 us (98%)
  local copies, waits for them, and re-layouts  0.97 us (1%)
    pallas_call x1, Pallas kernels, per_device(): pl.pallas_call(kernel, out_shape=pltpu.VMEM(queries.shape, BF16), in_spec...  70.6 us

profile of v6, /device:TPU:25, one launch (start us, length us, event | category | flops | bytes accessed | tf_op | source)
XLA Modules:
  0.0 71.6 jit_solution(13177289799379958151)
XLA Ops:
  0.0 70.6 %causal_attention.1 = bf16[128,4096]{1,0:T(8,128)(2,1)S(1)} custom-call(bf16[128,4096]{1,0:T(8,128)(2,1)} %q_ref.1, bf16[128,1024]{1,0:T(8,128)(2,1)} %k_ref.1, bf16[128,1024]{1,0:T(8,128)(2,1)} %v_ref.1), custom_call_target="tpu_custom_call" | custom-call | tf_op jit(solution)/shard_map/causal_attention/pallas_call | solution.py:478
  70.6 1.0 %copy.5 = bf16[128,4096]{1,0:T(8,128)(2,1)} copy(bf16[128,4096]{1,0:T(8,128)(2,1)S(1)} %causal_attention.1) | data formatting | bytes 2097152

commit v7 on v6

--- a/solution.py
+++ b/solution.py
@@ -224,7 +224,7 @@
         return [blocks[i : i + size // BLOCK] for i in range(0, len(blocks), size // BLOCK)]
 
     def from_pairs(pairs):
-        return [(chunk, 4 * c_ + 2 * mz + hz) for chunk, mz in pairs for c_ in range(2) for hz in range(2)]
+        return [(chunk, 4 * c_ + 2 * mz + hz) for c_ in (c, 1 - c) for chunk, mz in pairs for hz in range(2)]
 
     def work(ahead, behind, after_span=None):
         ahead_parts = parts(ahead[1], AHEAD) if ahead else []
@@ -280,7 +280,7 @@
         for h in range(span * SPAN // BLOCK, (span + 1) * SPAN // BLOCK):
             columns_ = slice(h * BLOCK, (h + 1) * BLOCK)
             part = acc[slot, :, columns_] * (1.0 / jnp.sum(total[slot, :, columns_], axis=0, keepdims=True))
-            o_buf[slot, :, h * WIDTH : (h + 1) * WIDTH] = part.T.astype(BF16)
+            o_buf[slot, :, h * WIDTH : (h + 1) * WIDTH] = part.astype(BF16).T
         src, dst = result(slot, span)
 
         @pl.when(slot != my_slot)
@@ -317,7 +317,6 @@
     pl.when(high_y == 1)(send_kv)
     split_queries(4)
     split_queries(5)
-    own_twin_1(0)
 
     def side_of(k):
         return lax.rem(high_z + 3 - k, 2)
@@ -392,7 +391,18 @@
 
     a, b = (score_a, top_a), (score_b, top_b)
     zero = jnp.int32(0)
-    work((*whole(unit(zero, zero)), *a, None), None)
+    slot_0, blocks_0 = whole(unit(zero, zero))
+    for part in range(2):
+        if part == 1:
+            own_twin_1(0)
+        keys_0 = jnp.concatenate([kv[chunk, row, 0] for chunk, row in blocks_0[8 * part : 8 * part + 8]], axis=0)
+        keys_0 = jnp.concatenate([keys_0, keys_0], axis=1)
+        for start in range(0, ROWS, SPAN):
+            columns_0 = slice(start, start + SPAN)
+            s_0 = lax.dot_general(keys_0, q_pair[slot_0, columns_0], (((1,), (1,)), ((), ())), preferred_element_type=F32)
+            score_a[CHUNK * part : CHUNK * (part + 1), columns_0] = s_0
+            best = jnp.max(s_0.reshape(-1, 8, SPAN), axis=0)
+            top_a[:, columns_0] = jnp.maximum(top_a[:, columns_0], best) if part else best
 
     def full(r, i, _):
         for step, actions in steps.items():

time: 71.9 us -> 71.8 us (level)
  no operation moved by 1% of the time
where the time goes in v7:
time: 71.8 us; the launch traced here: 71.4 us
  Pallas kernels  70.4 us (98%)
  local copies, waits for them, and re-layouts  0.97 us (1%)
    pallas_call x1, Pallas kernels, per_device(): pl.pallas_call(kernel, out_shape=pltpu.VMEM(queries.shape, BF16), in_spec...  70.4 us

profile of v7, /device:TPU:25, one launch (start us, length us, event | category | flops | bytes accessed | tf_op | source)
XLA Modules:
  0.0 71.4 jit_solution(8681658531689198206)
XLA Ops:
  0.0 70.4 %causal_attention.1 = bf16[128,4096]{1,0:T(8,128)(2,1)S(1)} custom-call(bf16[128,4096]{1,0:T(8,128)(2,1)} %q_ref.1, bf16[128,1024]{1,0:T(8,128)(2,1)} %k_ref.1, bf16[128,1024]{1,0:T(8,128)(2,1)} %v_ref.1), custom_call_target="tpu_custom_call" | custom-call | tf_op jit(solution)/shard_map/causal_attention/pallas_call | solution.py:488
  70.4 1.0 %copy.5 = bf16[128,4096]{1,0:T(8,128)(2,1)} copy(bf16[128,4096]{1,0:T(8,128)(2,1)S(1)} %causal_attention.1) | data formatting | bytes 2097152
